TPU v7x, 128 devices: a whole 4x4x4 slice. The times are simulated.
128 devices in a mesh: mpo: 4 (over x), bond: 32 (over y, z, core).
Axes of the slice: x: 4, y: 4, z: 4, core: 2. Of those that a mesh axis runs over, the one named last changes fastest.
Arguments:
- wavefunction: bfloat16 [4096, 4096], P('bond'), may hold values from -44 to 44
- subspace: bfloat16 [4, 4096, 4096], P(None, 'mpo', 'bond'), may hold values from -110 to 110
- left_band: bfloat16 [36, 4096, 320], P('mpo', 'bond'), may hold values from -3 to 3
- right_band: bfloat16 [36, 4096, 320], P('mpo', 'bond'), may hold values from -1 to 1
- left_sector: int32 [64], replicated, may hold values from 0 to 31, never falling along the last dimension, each value on 1 to 3 neighbouring positions
- right_sector: int32 [64], replicated, may hold values from 0 to 31, never falling along the last dimension, each value on 1 to 3 neighbouring positions
- term_sectors: int32 [36, 32], P('mpo'), may hold values 0 or 1
Outputs:
- applied: float32 [4096, 4096], P('mpo', 'bond')
- new_vector: float32 [4096, 4096], P('mpo', 'bond')
Inputs may be any that keep to these rules, and one draw needn't show every extreme that they name: left_sector never falls; each sector covers 1 to 3 consecutive tiles, one exactly 3. right_sector never falls; each sector covers 1 to 3 consecutive tiles, one exactly 3.
All inputs are finite; a program needn't handle non-finite values. No bound on the sum of `term_sectors` on one device may be relied on, other than what follows from the above.
Results may differ from a plain program's by a relative error of at most 0.0023.
Values may be sent and summed in bfloat16 or wider, within the bound.
A program may use at most 128 MiB of HBM per device.

v0:
```python
import jax
import jax.numpy as jnp
from jax import lax
from jax.sharding import PartitionSpec as P

D_LEFT = 4096
D_RIGHT = 4096
TILE = 64
SEC_MOST = 3


epsilon = 1e-06


def extended(cells, sides, width):
    for axis, dim in sides:
        count = lax.axis_size(axis)
        ends = count - 1
        head = lax.slice_in_dim(cells, 0, width, axis=dim)
        tail = lax.slice_in_dim(cells, cells.shape[dim] - width, cells.shape[dim], axis=dim)
        cells = jnp.concatenate(
            [
                lax.ppermute(tail, axis, [(i, (i + 1) % count) for i in range(ends)]),
                cells,
                lax.ppermute(head, axis, [((i + 1) % count, i) for i in range(ends)]),
            ],
            axis=dim,
        )
    return cells


def padded_sectors(sector, margin):
    filler = -jnp.ones((margin,), jnp.int32)
    return jnp.concatenate([filler, sector, filler])


def left_section(bands, source, active_tiles, left_sector, tile_count):
    margin = SEC_MOST - 1
    spans = 2 * margin + 1
    groups = bands.shape[0]
    columns = source.shape[1]
    window = padded_sectors(left_sector, margin)
    own_sector = window[margin : margin + tile_count]
    switched = (active_tiles > 0).astype(jnp.float32)
    tiled_rows = source.reshape(tile_count + 2 * margin, TILE, columns)
    linked = jnp.stack(
        [window[offset : offset + tile_count] == own_sector for offset in range(spans)], axis=1
    ).astype(jnp.bfloat16)
    stacked = jnp.stack(
        [tiled_rows[offset : offset + tile_count] for offset in range(spans)], axis=1
    )
    stacked = (stacked * linked[:, :, None, None]).reshape(tile_count, spans * TILE, columns)
    blocks = bands.reshape(groups, tile_count, TILE, spans * TILE)
    running = jnp.einsum("wtib,tbc->wtic", blocks, stacked, preferred_element_type=jnp.float32)
    running = running * switched[:, :, None, None]
    return running.reshape(groups, tile_count * TILE, columns).astype(jnp.bfloat16)


def per_device(
    wavefunction, subspace, left_band, right_band, left_sector, right_sector, term_sectors
):
    margin = SEC_MOST - 1
    spans = 2 * margin + 1
    halo_width = margin * TILE
    groups = left_band.shape[0]
    position = lax.axis_index("bond")
    sector_range = jnp.arange(term_sectors.shape[1], dtype=jnp.int32)
    member = (left_sector[:, None] == sector_range[None, :]).astype(jnp.int32)
    active_tiles = jnp.sum(term_sectors[:, None, :] * member[None, :, :], axis=2)
    local_columns = lax.all_to_all(wavefunction, "bond", split_axis=1, concat_axis=0, tiled=True)
    all_bands = lax.all_gather(left_band, "bond", axis=1, tiled=True)
    zero_rows = jnp.zeros((halo_width, local_columns.shape[1]), jnp.bfloat16)
    source = jnp.concatenate([zero_rows, local_columns, zero_rows])
    middle = left_section(all_bands, source, active_tiles, left_sector, D_LEFT // TILE)
    columns = right_band.shape[1]
    column_tiles = columns // TILE
    window = lax.dynamic_slice_in_dim(
        padded_sectors(right_sector, margin), position * column_tiles, column_tiles + 2 * margin
    )
    own_sector = window[margin : margin + column_tiles]
    rows_all = middle.shape[1]
    tiled_middle = middle.reshape(groups, rows_all, column_tiles, TILE)
    blocks = right_band.reshape(groups, column_tiles, TILE, spans * TILE)
    linked = jnp.stack(
        [window[offset : offset + column_tiles] == own_sector for offset in range(spans)], axis=1
    ).astype(jnp.float32)
    products = jnp.einsum(
        "wrjc,wjcb->rjb", tiled_middle, blocks, preferred_element_type=jnp.float32
    )
    products = products.reshape(rows_all, column_tiles, spans, TILE) * linked[None, :, :, None]
    spread = jnp.pad(products[:, :, 0], ((0, 0), (0, 2 * margin), (0, 0)))
    for offset in range(1, spans):
        spread = spread + jnp.pad(
            products[:, :, offset], ((0, 0), (offset, 2 * margin - offset), (0, 0))
        )
    outer_parts = jnp.concatenate(
        [spread[:, :margin], spread[:, margin + column_tiles :]], axis=1
    ).reshape(rows_all, 2 * halo_width)
    received = extended(outer_parts, (("bond", 1),), halo_width)
    centre = spread[:, margin : margin + column_tiles].reshape(rows_all, columns)
    centre = centre.at[:, :halo_width].add(received[:, :halo_width])
    centre = centre.at[:, columns - halo_width :].add(received[:, 3 * halo_width :])
    applied = lax.psum_scatter(centre, "mpo", scatter_dimension=0, tiled=True)
    entries = D_LEFT * D_RIGHT
    highest = lax.Precision.HIGHEST
    local_correlation = jnp.einsum(
        "kxy,xy->k", subspace, applied, precision=highest, preferred_element_type=jnp.float32
    )
    local_square = jnp.einsum("kxy,kxy->k", subspace, subspace, preferred_element_type=jnp.float32)
    correlation, squares = lax.psum((local_correlation, local_square), ("mpo", "bond"))
    coefficient = correlation / entries / (squares / entries + epsilon)
    residual = applied - jnp.einsum(
        "k,kxy->xy", coefficient, subspace, precision=highest, preferred_element_type=jnp.float32
    )
    energy = lax.psum(jnp.sum(residual * residual), ("mpo", "bond"))
    new_vector = residual * lax.rsqrt(energy / entries + epsilon)
    return (applied, new_vector)


def solution(mesh):
    return jax.shard_map(
        per_device,
        mesh=mesh,
        in_specs=(
            P("bond", None),
            P(None, "mpo", "bond"),
            P("mpo", "bond", None),
            P("mpo", "bond", None),
            P(),
            P(),
            P("mpo", None),
        ),
        out_specs=(P("mpo", "bond"), P("mpo", "bond")),
        check_vma=False,
    )
```

profile of v0, /device:TPU:1, one launch (start us, length us, event | category | flops | bytes accessed | tf_op | source)
XLA Modules:
  0.0 426.8 jit_solution(10889323196408372372)
XLA Ops:
  7.3 2.3 copy.45
  9.6 2.3 copy.40
  11.8 9.6 %all-to-all-start = ((bf16[128,32,128]{0,2,1:T(8,128)(2,1)}), bf16[128,32,128]{0,2,1:T(8,128)(2,1)S(1)}, u32[]{:S(2)}, u32[]{:S(2)}) async-start(bf16[128,32,128]{0,2,1:T(8,128)(2,1)} %bitcast), calls=%async_computation | async-start | bytes 2097152 | tf_op jit(solution)/shard_map/all_to_all | solution.py:70
  21.5 0.1 multiply_reduce_fusion.1
  21.7 0.1 copy.47
  21.7 0.1 compare_bitcast_fusion.4
  21.9 0.1 copy.44
  22.0 1.1 copy.49
  23.2 0.1 pad_add_fusion.1
  23.2 0.1 dynamic_slice.3
  23.3 0.1 compare_bitcast_fusion
  23.4 22.1 %all-to-all-done = bf16[128,32,128]{0,2,1:T(8,128)(2,1)S(1)} async-done(((bf16[128,32,128]{0,2,1:T(8,128)(2,1)}), bf16[128,32,128]{0,2,1:T(8,128)(2,1)S(1)}, u32[]{:S(2)}, u32[]{:S(2)}) %all-to-all-start) | async-done | bytes 1048608 | tf_op jit(solution)/shard_map/all_to_all | solution.py:70
  45.5 0.7 copy.41
  46.2 0.5 pad_slice_fusion
  46.7 0.1 constant_dynamic-update-slice_fusion.4
  46.8 0.1 constant_dynamic-update-slice_fusion.3
  46.9 0.1 constant_dynamic-update-slice_fusion.2
  47.1 0.1 constant_dynamic-update-slice_fusion.1
  47.2 0.1 constant_dynamic-update-slice_fusion
  47.4 1.2 copy.43
  48.6 5.2 %bitcast_multiply_fusion.1 = bf16[64,320,128]{2,1,0:T(8,128)(2,1)} fusion(bf16[64,5,64,128]{3,2,1,0:T(8,128)(2,1)S(1)} %copy.43, bf16[64,320]{1,0:T(8,128)(2,1)S(1)} %copy.44), kind=kLoop, calls=%fused_computation.7 | loop fusion | flops 2621440 | bytes 10526720 | tf_op jit(solution)/shard_map/mul | solution.py:52
  53.8 68.2 %all-gather.2.cloned.1.call-done = bf16[9,4096,320]{2,1,0:T(8,128)(2,1)} async-done(((bf16[9,128,320]{2,1,0:T(8,128)(2,1)}), bf16[9,4096,320]{2,1,0:T(8,128)(2,1)}) %all-gather.2.cloned.1.call-update) | async-done | bytes 23592976 | tf_op jit(solution)/shard_map/all_gather | solution.py:71
  122.1 17.8 %fusion.2 = bf16[9,64,64,128]{3,2,0,1:T(8,128)(2,1)} fusion(f32[9,64]{0,1:T(8,128)S(1)} %copy.47, bf16[9,64,64,320]{3,2,1,0:T(8,128)(2,1)} %bitcast.89, bf16[64,320,128]{2,1,0:T(8,128)(2,1)} %bitcast_multiply_fusion.1), kind=kOutput, calls=%fused_computation.3 | convolution fusion | flops 3029336064 | bytes 38275328 | tf_op jit(solution)/shard_map/wtib,tbc->wtic/dot_general | solution.py:54
  139.9 26.8 %copy.48 = bf16[9,64,64,128]{2,1,3,0:T(8,128)(2,1)} copy(bf16[9,64,64,128]{3,2,0,1:T(8,128)(2,1)} %fusion.2) | data formatting | bytes 18874368 | tf_op jit(solution)/shard_map/convert_element_type | solution.py:56
  166.7 24.9 %convert_element_type.49 = bf16[9,4096,2,64]{1,3,2,0:T(8,128)(2,1)} reshape(bf16[9,64,64,128]{2,1,3,0:T(8,128)(2,1)} %copy.48) | data formatting | bytes 18874368 | tf_op jit(solution)/shard_map/convert_element_type | solution.py:56
  191.6 12.0 %fusion.20 = f32[2,4096,320,1]{1,2,0,3:T(8,128)} fusion(bf16[9,4096,2,64]{1,3,2,0:T(8,128)(2,1)} %convert_element_type.49, bf16[9,2,64,320]{3,2,1,0:T(8,128)(2,1)S(1)} %bitcast.87), kind=kOutput, calls=%fused_computation.55 | convolution fusion | flops 3019898880 | bytes 20660224 | tf_op jit(solution)/shard_map/wrjc,wjcb->rjb/dot_general | solution.py:87
  203.6 5.0 %copy_multiply_fusion = f32[4096,2,5,64]{0,3,1,2:T(8,128)S(1)} fusion(f32[4096,2,5,64]{0,3,2,1:T(8,128)} %bitcast.77, f32[2,5]{0,1:T(8,128)S(1)} %convert_element_type.50), kind=kLoop, calls=%fused_computation.4 | loop fusion | flops 2621440 | bytes 20971560 | tf_op jit(solution)/shard_map/mul | solution.py:90
  208.7 3.5 slice_bitcast_fusion.4
  212.2 3.7 pad_add_fusion
  215.9 0.6 fusion.18
  216.5 0.3 pad_maximum_fusion
  216.8 0.3 fusion.19
  217.1 2.2 collective-permute-start.1
  219.3 3.4 collective-permute-start
  222.7 21.8 %collective-permute-done.1 = f32[4096,128]{0,1:T(8,128)S(1)} collective-permute-done((f32[4096,128]{0,1:T(8,128)S(1)}, f32[4096,128]{0,1:T(8,128)S(1)}, u32[]{:S(2)}, u32[]{:S(2)}) %collective-permute-start.1) | collective-permute-done | bytes 2097184 | tf_op jit(solution)/shard_map/ppermute | solution.py:25
  244.5 1.2 collective-permute-done
  245.7 1.9 fusion.7
  247.6 0.4 fusion.6
  247.9 31.2 %reduce-scatter.2.cloned.1.call-done = f32[1024,128]{0,1:T(8,128)} async-done(((f32[4096,128]{0,1:T(8,128)}), f32[1024,128]{0,1:T(8,128)}) %reduce-scatter.2.cloned.1.call-update) | async-done | bytes 524304 | tf_op jit(solution)/shard_map/reduce_scatter | solution.py:103
  279.1 1.3 copy.54
  280.4 4.6 %convolution_bitcast_fusion = f32[4]{0:T(128)S(1)} fusion(f32[1024,128,1]{1,2,0:T(1,128)S(1)} %copy.54, bf16[4,1024,128]{2,1,0:T(8,128)(2,1)S(1)} %copy-done.1), kind=kOutput, calls=%fused_computation.18 | convolution fusion | flops 6291456 | bytes 1572880 | tf_op jit(solution)/shard_map/kxy,xy->k/dot_general | solution.py:106
  285.0 64.9 %all-reduce.9 = (f32[4]{0:T(128)S(1)}, f32[4]{0:T(128)S(1)}) all-reduce(f32[4]{0:T(128)S(1)} %fusion.6, f32[4]{0:T(128)S(1)} %convolution_bitcast_fusion), channel_id=1, replica_groups=mesh['mpo'=4,'bond'=32] {'mpo','bond'}, use_global_device_ids=true, to_apply=%region_3.4 | all-reduce | flops 8 | bytes 64 | tf_op jit(solution)/shard_map/psum | solution.py:110
  349.9 2.0 fusion.8
  351.9 0.3 copy.59
  352.3 0.8 multiply_reduce_fusion
  353.0 64.1 %psum.23 = f32[]{:T(128)} all-reduce(f32[]{:T(128)} %multiply_reduce_fusion), channel_id=1, replica_groups=mesh['mpo'=4,'bond'=32] {'mpo','bond'}, use_global_device_ids=true, to_apply=%region_5.6 | all-reduce | flops 1 | bytes 8 | tf_op jit(solution)/shard_map/psum | solution.py:115
  417.9 1.0 copy.52
  418.9 1.0 copy.51
  (27 shorter events, 0.3 us)
Async XLA Ops:
  7.2 14.3 %copy-start.4 = (s32[64]{0:T(128)S(1)}, s32[64]{0:T(128)}, u32[]{:S(2)}) copy-start(s32[64]{0:T(128)} %param.19) | copy-start | bytes 772
  7.2 14.3 %copy-start.3 = (s32[9,32]{1,0:T(8,128)S(1)}, s32[9,32]{1,0:T(8,128)}, u32[]{:S(2)}) copy-start(s32[9,32]{1,0:T(8,128)} %param.21) | copy-start | bytes 3460
  7.2 14.8 %copy-start.2 = (bf16[9,128,320]{1,2,0:T(8,128)(2,1)S(1)}, bf16[9,128,320]{1,2,0:T(8,128)(2,1)}, u32[]{:S(2)}) copy-start(bf16[9,128,320]{1,2,0:T(8,128)(2,1)} %param.18) | copy-start | bytes 2211844
  7.2 15.9 %copy-start.5 = (s32[64]{0:T(128)S(1)}, s32[64]{0:T(128)}, u32[]{:S(2)}) copy-start(s32[64]{0:T(128)} %param.20) | copy-start | bytes 772
  7.2 114.9 %all-gather.2.cloned.1.call-start = ((), (), s32[]{:S(2)}) async-start(), calls=%async_computation.2 | async-start | bytes 29196288 | tf_op jit(solution)/shard_map/all_gather | solution.py:71
  11.8 33.7 %all-to-all-start = ((bf16[128,32,128]{0,2,1:T(8,128)(2,1)}), bf16[128,32,128]{0,2,1:T(8,128)(2,1)S(1)}, u32[]{:S(2)}, u32[]{:S(2)}) async-start(bf16[128,32,128]{0,2,1:T(8,128)(2,1)} %bitcast), calls=%async_computation | async-start | bytes 2097152 | tf_op jit(solution)/shard_map/all_to_all | solution.py:70
  21.4 257.7 %reduce-scatter.2.cloned.1.call-start = ((), (), s32[]{:S(2)}) async-start(), calls=%async_computation.3 | async-start | bytes 2621440 | tf_op jit(solution)/shard_map/reduce_scatter | solution.py:103
  217.1 27.4 %collective-permute-start.1 = (f32[4096,128]{0,1:T(8,128)S(1)}, f32[4096,128]{0,1:T(8,128)S(1)}, u32[]{:S(2)}, u32[]{:S(2)}) collective-permute-start(f32[4096,128]{0,1:T(8,128)S(1)} %get-tuple-element.59), channel_id=1, source_target_pairs={{1,0},{2,1},{3,2},{4,3},{5,4},{6,5},{7,6},{8,7},{9,8},{10,9},{11,1... | collective-permute-start | bytes 6291464 | tf_op jit(solution)/shard_map/ppermute | solution.py:25
  219.3 26.4 %collective-permute-start = (f32[4096,128]{0,1:T(8,128)S(1)}, f32[4096,128]{0,1:T(8,128)S(1)}, u32[]{:S(2)}, u32[]{:S(2)}) collective-permute-start(f32[4096,128]{0,1:T(8,128)S(1)} %get-tuple-element.58), channel_id=1, source_target_pairs={{0,1},{1,2},{2,3},{3,4},{4,5},{5,6},{6,7},{7,8},{8,9},{9,10},{10,1... | collective-permute-start | bytes 6291464 | tf_op jit(solution)/shard_map/ppermute | solution.py:23
  245.7 1.9 copy-start.1
  279.1 73.2 %copy-start = (f32[1024,128]{0,1:T(8,128)S(1)}, f32[1024,128]{0,1:T(8,128)}, u32[]{:S(2)}) copy-start(f32[1024,128]{0,1:T(8,128)} %reduce-scatter.2.cloned.1.call-done) | copy-start | bytes 1572868
Sparse Core Ops, SparseCore 0:
  10.3 111.7 all-gather.1
  247.7 31.3 reduce-scatter.1
where the time goes:
time: 428 us; the launch traced here: 427 us
  waiting for transfers between devices  144 us (34%)
  blocking collectives  129 us (30%)
  local copies, waits for them, and re-layouts  68.9 us (16%)
  matrix products  36.4 us (9%)
  other arithmetic  17.7 us (4%)
  starting transfers between devices  15.2 us (4%)
  between operations  15 us (4%)
    all_gather x1, waiting for transfers between devices, per_device(): all_bands = lax.all_gather(left_band, 'bond', axis=1, tiled=True)  68.2 us
    psum x1, blocking collectives, per_device(): lax.psum((local_correlation, local_square), ('mpo', 'bond'))  64.9 us
    psum x1, blocking collectives, per_device(): energy = lax.psum(jnp.sum(residual * residual), ('mpo', 'bond'))  64.1 us
    convert_element_type x2, local copies, waits for them, and re-layouts, left_section(): running.reshape(groups, tile_count * TILE, columns).astype(jnp.bfloat16)  51.7 us
    reduce_scatter x1, waiting for transfers between devices, per_device(): applied = lax.psum_scatter(centre, 'mpo', scatter_dimension=0, tiled=True)  31.2 us
    all_to_all x1, waiting for transfers between devices, per_device(): lax.all_to_all(wavefunction, 'bond', split_axis=1, concat_axis=0, tiled=T...  22.1 us
    ppermute x1, waiting for transfers between devices, extended(): lax.ppermute(head, axis, [((i + 1) % count, i) for i in range(ends)])  21.8 us
    dot_general x1, matrix products, left_section(): jnp.einsum('wtib,tbc->wtic', blocks, stacked, preferred_element_type=jnp....  17.8 us
  transfers between devices with their start and end apart: 5, of which 5 were waited for; matrix products, arithmetic and copies ran while one was open for 3% of the time, Pallas kernels for 0%

commit v1 on v0

v1 whole, which is shorter than its diff:
```python
import jax
import jax.numpy as jnp
from jax import lax
from jax.experimental import pallas as pl
from jax.experimental.pallas import tpu as pltpu
from jax.sharding import PartitionSpec as P

D_LEFT = 4096
D_RIGHT = 4096
TILE = 64
SEC_MOST = 3
MARGIN = SEC_MOST - 1
SPANS = 2 * MARGIN + 1
PACKED = SEC_MOST * TILE
NT = D_RIGHT // TILE
CHUNKS = 3
MESH = pl.DeviceIdType.MESH

epsilon = 1e-06


def sector_starts(sector):
    same = sector[:, None] == sector[None, :]
    return jnp.argmax(same, axis=1).astype(jnp.int32)


def pack_kernel(place_ref, band_ref, mask_ref, out_ref):
    groups = band_ref.shape[0]
    for w in range(groups):
        halves = []
        for h in range(2):
            rows = band_ref[w, h * TILE : (h + 1) * TILE, :]
            p = place_ref[h]
            picked = jnp.where(
                p == 0,
                rows[:, 2 * TILE : 2 * TILE + PACKED],
                jnp.where(p == 1, rows[:, TILE : TILE + PACKED], rows[:, :PACKED]),
            )
            halves.append(picked * mask_ref[h : h + 1, :PACKED])
        out_ref[w] = jnp.concatenate(halves, axis=1)


def left_kernel(band_ref, mask_ref, prev_ref, own_ref, next_ref, out_ref, kept_ref):
    groups = band_ref.shape[0]

    @pl.when(pl.program_id(0) == 0)
    def _():
        for w in range(groups):
            for h in range(2):
                kept_ref[h, w * TILE : (w + 1) * TILE, :] = (
                    band_ref[w, h * TILE : (h + 1) * TILE, :] * mask_ref[w, h : h + 1, :]
                )

    rows = jnp.concatenate([prev_ref[...], own_ref[...], next_ref[...]], axis=0)
    for h in range(2):
        made = jnp.dot(
            kept_ref[h],
            rows[h * TILE : h * TILE + SPANS * TILE],
            preferred_element_type=jnp.float32,
        ).astype(jnp.bfloat16)
        for w in range(groups):
            out_ref[w, h * TILE : (h + 1) * TILE, :] = made[w * TILE : (w + 1) * TILE]


def right_kernel(blocks_each, first, start_ref, mid_ref, band_ref, *rest):
    if first:
        out_ref, total = rest
    else:
        part_ref, out_ref, total = rest
    step = pl.program_id(0)

    @pl.when(step == 0)
    def _():
        total[...] = jnp.zeros_like(total) if first else part_ref[...]

    terms = mid_ref.shape[0]
    lane = lax.broadcasted_iota(jnp.int32, (128, 256), 1)
    for b in range(blocks_each):
        for h in range(2):
            left = jnp.concatenate(
                [
                    mid_ref[w, :, b * 128 + h * TILE : b * 128 + (h + 1) * TILE]
                    for w in range(terms)
                ],
                axis=1,
            )
            right = band_ref[b, :, :, h * 128 : h * 128 + 256].reshape(terms * TILE, 256)
            made = jnp.dot(left, right, preferred_element_type=jnp.float32)
            start = start_ref[(step * blocks_each + b) * 2 + h]
            odd = lax.rem(start, 2)
            if h == 0:
                made = jnp.where(lane < PACKED, made, 0.0)
            else:
                made = jnp.where(lane >= TILE, made, 0.0)
            moved = pltpu.roll(made, TILE if h == 0 else 256 - TILE, 1)
            made = jnp.where(odd == h, made, moved)
            at = pl.ds(pl.multiple_of((start // 2) * 128, 128), 256)
            total[:, at] += made

    @pl.when(step == pl.num_programs(0) - 1)
    def _():
        out_ref[...] = total[...]


def finish_kernel(
    part_ref, sub_ref, applied_ref, vector_ref,
    out_a, in_a, out_b, app, mine, first_in, second_out, second_in,
    send_a, recv_a, send_b, recv_b, send_c, recv_c, send_d, recv_d,
):
    x = lax.axis_index("mpo")
    bond = lax.axis_index("bond")
    y = bond // 8
    q = lax.rem(bond, 8)

    barrier = pltpu.get_barrier_semaphore()
    for d in range(1, 8):
        pl.semaphore_signal(
            barrier, inc=1, device_id=(x, y * 8 + lax.rem(q + d, 8)), device_id_type=MESH
        )
    for d in range(1, 16):
        other = lax.rem(x * 4 + y + d, 16)
        pl.semaphore_signal(
            barrier, inc=1, device_id=(other // 4, lax.rem(other, 4) * 8 + q), device_id_type=MESH
        )

    @pl.when(x != y)
    def _():
        for k in range(8):
            pl.semaphore_signal(barrier, inc=1, device_id=(y, x * 8 + k), device_id_type=MESH)
        pl.semaphore_wait(barrier, 30)

    @pl.when(x == y)
    def _():
        pl.semaphore_wait(barrier, 22)

    copies_a = []
    for d in range(1, 4):
        j = lax.rem(x + d, 4)
        columns = pl.ds(pl.multiple_of(j * 1024, 1024), 1024)
        out_a[d - 1] = part_ref[:, columns].astype(jnp.bfloat16)
        copy = pltpu.make_async_remote_copy(
            src_ref=out_a.at[d - 1], dst_ref=in_a.at[d - 1],
            send_sem=send_a.at[d - 1], recv_sem=recv_a.at[d - 1],
            device_id=(j, bond), device_id_type=MESH,
        )
        copy.start()
        copies_a.append(copy)

    mine[...] = jnp.zeros_like(mine)
    row = 5
    for k in range(4):
        for m in range(k, 4):
            def gram(i, held, k=k, m=m):
                at = pl.ds(pl.multiple_of(i * 64, 64), 64)
                return held + jnp.sum(
                    (sub_ref[k, at, :].astype(jnp.float32) * sub_ref[m, at, :].astype(jnp.float32)).reshape(8, 8, 128),
                    axis=0,
                )
            held = lax.fori_loop(0, 16, gram, jnp.zeros((8, 128), jnp.float32))
            mine[row : row + 1, :] = jnp.sum(held, axis=0, keepdims=True)
            row += 1

    for copy in copies_a:
        copy.wait()

    own = pl.multiple_of(x * 1024, 1024)
    for k in range(8):
        at = pl.ds(pl.multiple_of(own + k * 128, 128), 128)
        out_b[k] = (
            part_ref[:, at]
            + in_a[0, :, k * 128 : (k + 1) * 128].astype(jnp.float32)
            + in_a[1, :, k * 128 : (k + 1) * 128].astype(jnp.float32)
            + in_a[2, :, k * 128 : (k + 1) * 128].astype(jnp.float32)
        )
        here = (x == y) & (q == k)

        @pl.when(jnp.logical_not(here))
        def _(k=k):
            pltpu.make_async_remote_copy(
                src_ref=out_b.at[k], dst_ref=app.at[q],
                send_sem=send_b.at[k], recv_sem=recv_b.at[q],
                device_id=(y, x * 8 + k), device_id_type=MESH,
            ).start()

        @pl.when(here)
        def _(k=k):
            app[k] = out_b[k]

    for k in range(8):
        here = (x == y) & (q == k)

        @pl.when(jnp.logical_not(here))
        def _(k=k):
            pltpu.make_async_remote_copy(
                src_ref=out_b.at[k], dst_ref=app.at[k],
                send_sem=send_b.at[k], recv_sem=recv_b.at[k],
                device_id=(y, x * 8 + k), device_id_type=MESH,
            ).wait()

    def sums(i, held):
        block = app[i]
        rows = pl.ds(pl.multiple_of(i * 128, 128), 128)
        new = [held[0] + jnp.sum((block * block).reshape(16, 8, 128), axis=0)]
        for k in range(4):
            product = sub_ref[k, rows, :].astype(jnp.float32) * block
            new.append(held[k + 1] + jnp.sum(product.reshape(16, 8, 128), axis=0))
        return tuple(new)

    held = lax.fori_loop(0, 8, sums, tuple(jnp.zeros((8, 128), jnp.float32) for _ in range(5)))
    for k in range(5):
        mine[k : k + 1, :] = jnp.sum(held[k], axis=0, keepdims=True)

    copies = []
    for d in range(1, 8):
        copy = pltpu.make_async_remote_copy(
            src_ref=mine, dst_ref=first_in.at[d - 1],
            send_sem=send_c.at[d - 1], recv_sem=recv_c.at[d - 1],
            device_id=(x, y * 8 + lax.rem(q + d, 8)), device_id_type=MESH,
        )
        copy.start()
        copies.append(copy)
    for copy in copies:
        copy.wait()
    added = mine[...]
    for d in range(7):
        added = added + first_in[d]
    second_out[...] = added
    copies = []
    for d in range(1, 16):
        other = lax.rem(x * 4 + y + d, 16)
        copy = pltpu.make_async_remote_copy(
            src_ref=second_out, dst_ref=second_in.at[d - 1],
            send_sem=send_d.at[d - 1], recv_sem=recv_d.at[d - 1],
            device_id=(other // 4, lax.rem(other, 4) * 8 + q), device_id_type=MESH,
        )
        copy.start()
        copies.append(copy)
    for copy in copies:
        copy.wait()
    for d in range(15):
        added = added + second_in[d]
    sums_all = jnp.sum(added, axis=1, keepdims=True)

    entries = float(D_LEFT * D_RIGHT)

    def one(i):
        return sums_all[i : i + 1, :] * (1.0 / entries)

    gram_at = {}
    row = 5
    for k in range(4):
        for m in range(k, 4):
            gram_at[k, m] = row
            row += 1
    coefficient = [one(1 + k) / (one(gram_at[k, k]) + epsilon) for k in range(4)]
    energy = one(0)
    for k in range(4):
        energy = energy - 2.0 * coefficient[k] * one(1 + k)
        for m in range(k, 4):
            twice = 1.0 if m == k else 2.0
            energy = energy + twice * coefficient[k] * coefficient[m] * one(gram_at[k, m])
    scale = lax.rsqrt(jnp.maximum(energy, 0.0) + epsilon)

    def write(i, carry):
        rows = pl.ds(pl.multiple_of(i * 128, 128), 128)
        block = app[i]
        residual = block
        for k in range(4):
            residual = residual - coefficient[k] * sub_ref[k, rows, :].astype(jnp.float32)
        applied_ref[rows, :] = block
        vector_ref[rows, :] = residual * scale
        return carry

    lax.fori_loop(0, 8, write, 0)


def per_device(
    wavefunction, subspace, left_band, right_band, left_sector, right_sector, term_sectors
):
    groups = left_band.shape[0]
    position = lax.axis_index("bond")
    count = lax.axis_size("bond")
    ends = count - 1

    before = lax.ppermute(wavefunction, "bond", [(i, i + 1) for i in range(ends)])
    after = lax.ppermute(wavefunction, "bond", [(i + 1, i) for i in range(ends)])

    filler = -jnp.ones((SPANS,), jnp.int32)
    right_start = sector_starts(right_sector)
    own_tiles = position * 2 + jnp.arange(2, dtype=jnp.int32)
    own_start = right_start[own_tiles]
    place = own_tiles - own_start
    right_padded = jnp.concatenate([right_sector, filler])
    in_sector = jnp.stack(
        [right_padded[own_start + m] == right_sector[own_tiles] for m in range(SEC_MOST)], axis=1
    )
    pack_mask = jnp.repeat(in_sector.astype(jnp.bfloat16), TILE, axis=1)
    packed = pl.pallas_call(
        pack_kernel,
        out_shape=jax.ShapeDtypeStruct((groups, TILE, 2 * PACKED), jnp.bfloat16),
        in_specs=[
            pl.BlockSpec(memory_space=pltpu.SMEM),
            pl.BlockSpec(memory_space=pltpu.VMEM),
            pl.BlockSpec(memory_space=pltpu.VMEM),
        ],
        out_specs=pl.BlockSpec(memory_space=pltpu.VMEM),
        compiler_params=pltpu.CompilerParams(vmem_limit_bytes=32 * 1024 * 1024),
        name="pack_right",
    )(place, right_band, pack_mask)

    each = groups // CHUNKS
    gathered = [
        lax.all_gather(packed[i * each : (i + 1) * each], "bond", axis=0, tiled=False)
        for i in range(CHUNKS)
    ]

    left_padded = jnp.concatenate([filler, left_sector, filler])
    own_left = left_sector[own_tiles]
    linked = jnp.stack(
        [left_padded[SPANS + own_tiles + o - MARGIN] == own_left for o in range(SPANS)], axis=1
    )
    active = term_sectors[:, own_left] == 1
    left_mask = jnp.repeat(
        (linked[None] & active[:, :, None]).astype(jnp.bfloat16), TILE, axis=2
    )
    width = 512
    middle = pl.pallas_call(
        left_kernel,
        grid=(D_RIGHT // width,),
        out_shape=jax.ShapeDtypeStruct((groups, 128, D_RIGHT), jnp.bfloat16),
        in_specs=[
            pl.BlockSpec((groups, 128, SPANS * TILE), lambda i: (0, 0, 0)),
            pl.BlockSpec((groups, 2, SPANS * TILE), lambda i: (0, 0, 0)),
            pl.BlockSpec((128, width), lambda i: (0, i)),
            pl.BlockSpec((128, width), lambda i: (0, i)),
            pl.BlockSpec((128, width), lambda i: (0, i)),
        ],
        out_specs=pl.BlockSpec((groups, 128, width), lambda i: (0, 0, i)),
        scratch_shapes=[pltpu.VMEM((2, groups * TILE, SPANS * TILE), jnp.bfloat16)],
        compiler_params=pltpu.CompilerParams(vmem_limit_bytes=48 * 1024 * 1024),
        cost_estimate=pl.CostEstimate(
            flops=2 * groups * 128 * 320 * 4096, bytes_accessed=14 << 20, transcendentals=0
        ),
        name="left_apply",
    )(left_band, left_mask, before, wavefunction, after)

    blocks_each = 4
    held = D_RIGHT + 128
    part = None
    for i in range(CHUNKS):
        operands = [right_start, middle, gathered[i]]
        in_specs = [
            pl.BlockSpec(memory_space=pltpu.SMEM),
            pl.BlockSpec((each, 128, blocks_each * 128), lambda s, i=i: (i, 0, s)),
            pl.BlockSpec((blocks_each, each, TILE, 2 * PACKED), lambda s: (s, 0, 0, 0)),
        ]
        if part is not None:
            operands.append(part)
            in_specs.append(pl.BlockSpec((128, held), lambda s: (0, 0)))
        part = pl.pallas_call(
            lambda *refs, first=part is None: right_kernel(blocks_each, first, *refs),
            grid=(32 // blocks_each,),
            out_shape=jax.ShapeDtypeStruct((128, held), jnp.float32),
            in_specs=in_specs,
            out_specs=pl.BlockSpec((128, held), lambda s: (0, 0)),
            scratch_shapes=[pltpu.VMEM((128, held), jnp.float32)],
            compiler_params=pltpu.CompilerParams(vmem_limit_bytes=48 * 1024 * 1024),
            cost_estimate=pl.CostEstimate(
                flops=2 * 64 * 128 * 192 * 256, bytes_accessed=12 << 20, transcendentals=0
            ),
            name="right_apply",
        )(*operands)

    shape = jax.ShapeDtypeStruct((1024, 128), jnp.float32)
    dma = pltpu.SemaphoreType.DMA
    return pl.pallas_call(
        finish_kernel,
        out_shape=(shape, shape),
        in_specs=[pl.BlockSpec(memory_space=pltpu.VMEM)] * 2,
        out_specs=(pl.BlockSpec(memory_space=pltpu.VMEM),) * 2,
        scratch_shapes=[
            pltpu.VMEM((3, 128, 1024), jnp.bfloat16),
            pltpu.VMEM((3, 128, 1024), jnp.bfloat16),
            pltpu.VMEM((8, 128, 128), jnp.float32),
            pltpu.VMEM((8, 128, 128), jnp.float32),
            pltpu.VMEM((16, 128), jnp.float32),
            pltpu.VMEM((7, 16, 128), jnp.float32),
            pltpu.VMEM((16, 128), jnp.float32),
            pltpu.VMEM((15, 16, 128), jnp.float32),
            dma((3,)), dma((3,)), dma((8,)), dma((8,)),
            dma((7,)), dma((7,)), dma((15,)), dma((15,)),
        ],
        compiler_params=pltpu.CompilerParams(
            collective_id=0, has_side_effects=True, vmem_limit_bytes=32 * 1024 * 1024
        ),
        name="finish",
    )(part, subspace)


def solution(mesh):
    return jax.shard_map(
        per_device,
        mesh=mesh,
        in_specs=(
            P("bond", None),
            P(None, "mpo", "bond"),
            P("mpo", "bond", None),
            P("mpo", "bond", None),
            P(),
            P(),
            P("mpo", None),
        ),
        out_specs=(P("mpo", "bond"), P("mpo", "bond")),
        check_vma=False,
    )
```

time: 428 us -> 243 us (0.57)
  blocking collectives: 129 us -> 0 us
  Pallas kernels: 0 us -> 91.8 us
  local copies, waits for them, and re-layouts: 68.9 us -> 18.7 us
  matrix products: 36.4 us -> 0 us
  waiting for transfers between devices: 144 us -> 109 us
  other arithmetic: 17.7 us -> 1.8 us
  starting transfers between devices: 15.2 us -> 6.97 us
    psum x2 -> x0, blocking collectives: 129 us -> none  [the longest x1 64.9 us: per_device(): lax.psum((local_correlation, local_square), ('mpo', 'bond'))]
    pallas_call x0 -> x6, Pallas kernels: none -> 91.8 us  [the longest x1 55 us: per_device(): pl.pallas_call(finish_kernel, out_shape=(shape, shape), in_specs=[pl.Bloc...]
    convert_element_type x3 -> x0, local copies, waits for them, and re-layouts: 51.8 us -> none  [the longest x2 51.7 us: left_section(): running.reshape(groups, tile_count * TILE, columns).astype(jnp.bfloat16)]
    dot_general x4 -> x0, matrix products: 36.4 us -> none  [the longest x1 17.8 us: left_section(): jnp.einsum('wtib,tbc->wtic', blocks, stacked, preferred_element_type=jnp....]
    reduce_scatter x1 -> x0, waiting for transfers between devices: 31.2 us -> none  [per_device(): applied = lax.psum_scatter(centre, 'mpo', scatter_dimension=0, tiled=True)]
    all_gather x1 -> x3, waiting for transfers between devices: 68.2 us -> 98.5 us  [per_device(): lax.all_gather(packed[i * each:(i + 1) * each], 'bond', axis=0, tiled=False)]
    all_to_all x1 -> x0, waiting for transfers between devices: 22.1 us -> none  [per_device(): lax.all_to_all(wavefunction, 'bond', split_axis=1, concat_axis=0, tiled=T...]
    ppermute x2, waiting for transfers between devices: 23 us -> 9.26 us  [the longest x1 5.59 us: per_device(): lax.ppermute(wavefunction, 'bond', [(i + 1, i) for i in range(ends)])]
  transfers between devices with their start and end apart: 5 -> 5, of which waited for: 5 -> 5; matrix products, arithmetic and copies ran while one was open for 3% -> 3% of each run, Pallas kernels for 0% -> 11%
where the time goes in v1:
time: 243 us; the launch traced here: 242 us
  waiting for transfers between devices  109 us (45%)
  Pallas kernels  91.8 us (38%)
  local copies, waits for them, and re-layouts  18.7 us (8%)
  between operations  14 us (6%)
  starting transfers between devices  6.97 us (3%)
    all_gather x3, waiting for transfers between devices, per_device(): lax.all_gather(packed[i * each:(i + 1) * each], 'bond', axis=0, tiled=False)  98.5 us
    pallas_call x1, Pallas kernels, per_device(): pl.pallas_call(finish_kernel, out_shape=(shape, shape), in_specs=[pl.Bloc...  55 us
    pallas_call x3, Pallas kernels, per_device(): pl.pallas_call(lambda *refs, first=part is None: right_kernel(blocks_each...  25.4 us
    pallas_call x1, Pallas kernels, per_device(): pl.pallas_call(left_kernel, grid=(D_RIGHT // width,), out_shape=jax.Shape...  9.62 us
    unnamed x17, local copies, waits for them, and re-layouts  8.11 us
    ppermute x1, waiting for transfers between devices, per_device(): lax.ppermute(wavefunction, 'bond', [(i + 1, i) for i in range(ends)])  5.59 us
    ppermute x1, starting transfers between devices, per_device(): lax.ppermute(wavefunction, 'bond', [(i, i + 1) for i in range(ends)])  4.94 us
  transfers between devices with their start and end apart: 5, of which 5 were waited for; matrix products, arithmetic and copies ran while one was open for 3% of the time, Pallas kernels for 11%

profile of v1, /device:TPU:1, one launch (start us, length us, event | category | flops | bytes accessed | tf_op | source)
XLA Modules:
  0.0 242.4 jit_solution(2003812771207535420)
XLA Ops:
  7.3 1.4 iota_reduce_fusion
  8.7 1.3 gather_fusion.9
  10.0 0.6 gather_fusion.7
  10.7 0.7 concatenate.7
  11.3 0.6 gather_fusion.10
  12.0 0.6 gather_fusion.11
  12.6 0.6 gather_fusion.8
  13.3 0.1 copy.37
  13.4 0.1 copy.38
  13.5 0.1 copy.39
  13.6 0.1 add_convert_fusion
  13.7 0.1 reshape.247.mask_ref
  13.8 1.7 copy.40.band_ref
  15.6 1.8 pack_right.1
  17.4 0.8 fusion.10
  18.2 0.7 all-gather.9.cloned.1.call-update
  19.0 0.7 all-gather.7.cloned.1.call-update
  19.7 4.9 %collective-permute-start = (bf16[128,4096]{1,0:T(8,128)(2,1)S(1)}, bf16[128,4096]{1,0:T(8,128)(2,1)S(1)}, u32[]{:S(2)}, u32[]{:S(2)}) collective-permute-start(bf16[128,4096]{1,0:T(8,128)(2,1)S(1)} %copy-done.2), channel_id=1, source_target_pairs={{0,1},{1,2},{2,3},{3,4},{4,5},{5,6},{6,7},{7,8},{8,9},{9,10},{10,1... | collective-permute-start | bytes 3145736 | tf_op jit(solution)/shard_map/ppermute | solution.py:285
  24.6 1.9 collective-permute-start.1
  26.7 0.1 pad_add_fusion
  26.8 0.6 gather_fusion.1
  27.4 0.6 gather_fusion
  28.0 0.6 gather_fusion.2
  28.7 0.6 gather_fusion.3
  29.3 0.6 gather_fusion.4
  29.9 0.6 gather_fusion.5
  30.6 0.1 copy.33
  30.7 0.1 copy.34
  30.8 0.6 gather_fusion.6
  31.4 0.1 copy.35
  31.5 0.1 and_convert_fusion
  31.6 0.1 broadcast_in_dim.4
  31.7 0.1 reshape.246.mask_ref
  31.8 1.8 copy.36.band_ref
  33.6 3.7 %collective-permute-done.prev_ref = bf16[128,4096]{1,0:T(8,128)(2,1)S(1)} collective-permute-done((bf16[128,4096]{1,0:T(8,128)(2,1)S(1)}, bf16[128,4096]{1,0:T(8,128)(2,1)S(1)}, u32[]{:S(2)}, u32[]{:S(2)}) %collective-permute-start) | collective-permute-done | bytes 1048608 | tf_op jit(solution)/shard_map/ppermute | solution.py:285
  37.2 5.6 %collective-permute-done.1.next_ref = bf16[128,4096]{1,0:T(8,128)(2,1)} collective-permute-done((bf16[128,4096]{1,0:T(8,128)(2,1)S(1)}, bf16[128,4096]{1,0:T(8,128)(2,1)}, u32[]{:S(2)}, u32[]{:S(2)}) %collective-permute-start.1) | collective-permute-done | bytes 1048608 | tf_op jit(solution)/shard_map/ppermute | solution.py:286
  42.8 9.6 %left_apply.1.refs_1_ = bf16[9,128,4096]{2,1,0:T(8,128)(2,1)} custom-call(bf16[9,128,320]{2,1,0:T(8,128)(2,1)S(1)} %copy.36.band_ref, bf16[9,2,320]{2,1,0:T(2,128)(2,1)S(1)} %reshape.246.mask_ref, bf16[128,4096]{1,0:T(8,128)(2,1)S(1)} %collective-permute-done.prev_ref, bf16[128,4096]{1,0:T(8,128)(2,1)S(1)} %copy-done.2, ...), custom_call_target="tpu_custom_call" | custom-call | flops 3019898880 | bytes 14680064 | tf_op jit(solution)/shard_map/left_apply/pallas_call | solution.py:327
  52.5 19.1 %all-gather.11.cloned.1.call-done = bf16[96,64,384]{2,1,0:T(8,128)(2,1)} async-done(((bf16[3,64,384]{2,1,0:T(8,128)(2,1)}), bf16[96,64,384]{2,1,0:T(8,128)(2,1)}) %all-gather.11.cloned.1.call-update) | async-done | bytes 4718608 | tf_op jit(solution)/shard_map/all_gather | solution.py:313
  71.5 8.4 %right_apply.3.refs_3_ = f32[128,4224]{1,0:T(8,128)S(1)} custom-call(s32[64]{0:T(128)S(1)} %get-tuple-element.3.refs_0_, bf16[9,128,4096]{2,1,0:T(8,128)(2,1)} %left_apply.1.refs_1_, bf16[32,3,64,384]{3,2,1,0:T(8,128)(2,1)} %bitcast.62), custom_call_target="tpu_custom_call" | custom-call | flops 805306368 | bytes 12582912 | tf_op jit(solution)/shard_map/right_apply/pallas_call | solution.py:360
  80.0 40.7 %all-gather.9.cloned.1.call-done = bf16[96,64,384]{2,1,0:T(8,128)(2,1)} async-done(((bf16[3,64,384]{2,1,0:T(8,128)(2,1)}), bf16[96,64,384]{2,1,0:T(8,128)(2,1)}) %all-gather.9.cloned.1.call-update) | async-done | bytes 4718608 | tf_op jit(solution)/shard_map/all_gather | solution.py:313
  120.6 8.4 %right_apply.4.refs_3_ = f32[128,4224]{1,0:T(8,128)S(1)} custom-call(s32[64]{0:T(128)S(1)} %get-tuple-element.3.refs_0_, bf16[9,128,4096]{2,1,0:T(8,128)(2,1)} %left_apply.1.refs_1_, bf16[32,3,64,384]{3,2,1,0:T(8,128)(2,1)} %bitcast.63, f32[128,4224]{1,0:T(8,128)S(1)} %right_apply.3.refs_3_), custom_call_target="tpu_custom_call" | custom-call | flops 805306368 | bytes 12582912 | tf_op jit(solution)/shard_map/right_apply/pallas_call | solution.py:360
  129.1 1.3 copy-done
  130.4 38.8 %all-gather.7.cloned.1.call-done = bf16[96,64,384]{2,1,0:T(8,128)(2,1)} async-done(((bf16[3,64,384]{2,1,0:T(8,128)(2,1)}), bf16[96,64,384]{2,1,0:T(8,128)(2,1)}) %all-gather.7.cloned.1.call-update) | async-done | bytes 4718608 | tf_op jit(solution)/shard_map/all_gather | solution.py:313
  169.2 1.6 copy-done.1
  170.8 8.5 %right_apply.5.part_ref = f32[128,4224]{1,0:T(8,128)S(1)} custom-call(s32[64]{0:T(128)S(1)} %get-tuple-element.3.refs_0_, bf16[9,128,4096]{2,1,0:T(8,128)(2,1)} %left_apply.1.refs_1_, bf16[32,3,64,384]{3,2,1,0:T(8,128)(2,1)} %bitcast.64, f32[128,4224]{1,0:T(8,128)S(1)} %copy-done.1), custom_call_target="tpu_custom_call" | custom-call | flops 805306368 | bytes 12582912 | tf_op jit(solution)/shard_map/right_apply/pallas_call | solution.py:360
  179.3 55.0 %finish.1 = (f32[1024,128]{1,0:T(8,128)S(1)}, f32[1024,128]{1,0:T(8,128)S(1)}) custom-call(f32[128,4224]{1,0:T(8,128)S(1)} %right_apply.5.part_ref, bf16[4,1024,128]{2,1,0:T(8,128)(2,1)S(1)} %copy-done.3), custom_call_target="tpu_custom_call" | custom-call | tf_op jit(solution)/shard_map/finish/pallas_call | solution.py:376
  234.3 0.8 copy.43
  235.1 0.8 copy.44
  (36 shorter events, 0.4 us)
Async XLA Ops:
  7.2 12.5 %copy-start.2 = (bf16[128,4096]{1,0:T(8,128)(2,1)S(1)}, bf16[128,4096]{1,0:T(8,128)(2,1)}, u32[]{:S(2)}) copy-start(bf16[128,4096]{1,0:T(8,128)(2,1)} %own_ref.1) | copy-start | bytes 3145732
  7.2 19.5 %copy-start.4 = (s32[64]{0:T(128)S(1)}, s32[64]{0:T(128)}, u32[]{:S(2)}) copy-start(s32[64]{0:T(128)} %param.11) | copy-start | bytes 772
  7.2 64.4 %all-gather.11.cloned.1.call-start = ((), (), s32[]{:S(2)}) async-start(), calls=%async_computation.2 | async-start | bytes 4866048 | tf_op jit(solution)/shard_map/all_gather | solution.py:313
  10.0 20.8 %copy-start.5 = (s32[9,32]{1,0:T(8,128)S(1)}, s32[9,32]{1,0:T(8,128)}, u32[]{:S(2)}) copy-start(s32[9,32]{1,0:T(8,128)} %param.13) | copy-start | bytes 3460
  18.2 102.5 %all-gather.9.cloned.1.call-start = ((), (), s32[]{:S(2)}) async-start(), calls=%async_computation.1 | async-start | bytes 4866048 | tf_op jit(solution)/shard_map/all_gather | solution.py:313
  18.9 150.2 %all-gather.7.cloned.1.call-start = ((), (), s32[]{:S(2)}) async-start(), calls=%async_computation | async-start | bytes 4866048 | tf_op jit(solution)/shard_map/all_gather | solution.py:313
  19.7 17.6 %collective-permute-start = (bf16[128,4096]{1,0:T(8,128)(2,1)S(1)}, bf16[128,4096]{1,0:T(8,128)(2,1)S(1)}, u32[]{:S(2)}, u32[]{:S(2)}) collective-permute-start(bf16[128,4096]{1,0:T(8,128)(2,1)S(1)} %copy-done.2), channel_id=1, source_target_pairs={{0,1},{1,2},{2,3},{3,4},{4,5},{5,6},{6,7},{7,8},{8,9},{9,10},{10,1... | collective-permute-start | bytes 3145736 | tf_op jit(solution)/shard_map/ppermute | solution.py:285
  24.6 18.2 %collective-permute-start.1 = (bf16[128,4096]{1,0:T(8,128)(2,1)S(1)}, bf16[128,4096]{1,0:T(8,128)(2,1)}, u32[]{:S(2)}, u32[]{:S(2)}) collective-permute-start(bf16[128,4096]{1,0:T(8,128)(2,1)S(1)} %copy-done.2), channel_id=1, source_target_pairs={{1,0},{2,1},{3,2},{4,3},{5,4},{6,5},{7,6},{8,7},{9,8},{10,9},{11,1... | collective-permute-start | bytes 3145736 | tf_op jit(solution)/shard_map/ppermute | solution.py:286
  129.1 1.3 copy-start
  169.2 1.6 copy-start.1
  170.8 8.5 %copy-start.3 = (bf16[4,1024,128]{2,1,0:T(8,128)(2,1)S(1)}, bf16[4,1024,128]{2,1,0:T(8,128)(2,1)}, u32[]{:S(2)}) copy-start(bf16[4,1024,128]{2,1,0:T(8,128)(2,1)} %sub_ref.1) | copy-start | bytes 3145732
Sparse Core Ops, SparseCore 0:
  18.3 53.1 all-gather.10
  74.4 46.2 all-gather.8
  122.9 46.2 all-gather.6

commit v2 on v0

v2 whole, which is shorter than its diff:
```python
import functools

import jax
import jax.numpy as jnp
from jax import lax
from jax.experimental import pallas as pl
from jax.experimental.pallas import tpu as pltpu
from jax.sharding import PartitionSpec as P

D_LEFT = 4096
D_RIGHT = 4096
TILE = 64
SEC_MOST = 3
PACKED = SEC_MOST * TILE
NT = 64
TERMS = 9
DEEP = TERMS * TILE
MESH = pl.DeviceIdType.MESH

epsilon = 1e-06


def as_int(flag):
    return flag.astype(jnp.int32)


def place_in_sector(sector, tile):
    here = sector[tile]
    one = as_int((tile >= 1) & (sector[jnp.maximum(tile - 1, 0)] == here))
    two = as_int((tile >= 2) & (sector[jnp.maximum(tile - 2, 0)] == here))
    return one + two


def sector_size(sector, tile):
    here = sector[tile]
    one = as_int((tile <= NT - 2) & (sector[jnp.minimum(tile + 1, NT - 1)] == here))
    two = as_int((tile <= NT - 3) & (sector[jnp.minimum(tile + 2, NT - 1)] == here))
    return 1 + place_in_sector(sector, tile) + one + two


def pack(band, packed, sector, first_tile, active):
    lane = lax.broadcasted_iota(jnp.int32, (TILE, PACKED), 1)
    info = []
    for h in range(2):
        tile = first_tile + h
        info.append((place_in_sector(sector, tile), sector_size(sector, tile), sector[tile]))
    chosen = []
    if active is not None:
        number = lax.broadcasted_iota(jnp.int32, active.shape, 1)
        for h in range(2):
            same = 1 - jnp.clip(jnp.abs(number - info[h][2]), 0, 1)
            chosen.append(jnp.sum(active[...] * same, axis=1, keepdims=True))
    for w in range(TERMS):
        halves = []
        for h in range(2):
            p, size, here = info[h]
            rows = band[w, h * TILE : (h + 1) * TILE, :]
            limit = size * TILE
            if active is not None:
                limit = limit * chosen[h][w : w + 1]
            picked = 0.0
            for at in range(SEC_MOST):
                kept = jnp.clip(limit * as_int(p == at) - lane, 0, 1).astype(jnp.bfloat16)
                first = (SEC_MOST - 1 - at) * TILE
                picked = picked + rows[:, first : first + PACKED] * kept
            halves.append(picked)
        packed[w] = jnp.concatenate(halves, axis=1)


def kernel(
    lsec, rsec, terms, psi, sub, lband, rband,
    applied_ref, vector_ref,
    l_out, r_out, l_in, r_in, psi_in, r_ready, mid, out, halo_in, rs_out, rs_in, app,
    mine, first_in, second_out, second_in,
    psi1_s, psi1_r, psi2_s, psi2_r, r1_s, r1_r, r2_s, r2_r, l1_s, l2_s, l_r, lt_s, lt_r,
    halo_s, halo_r, rs_s, rs_r, send_c, recv_c, send_d, recv_d,
):
    x = lax.axis_index("mpo")
    bond = lax.axis_index("bond")
    y = bond // 8
    q = lax.rem(bond, 8)
    z = q // 2
    c = lax.rem(q, 2)

    def device(dx, dy, dz, dc):
        return (dx, dy * 8 + dz * 2 + dc)

    def turn(value, step):
        return lax.rem(value + step + 4, 4)

    def remote(src, dst, send, recv, target):
        return pltpu.make_async_remote_copy(
            src_ref=src, dst_ref=dst, send_sem=send, recv_sem=recv,
            device_id=target, device_id_type=MESH,
        )

    def arrived(dst, send, recv):
        remote(dst, dst, send, recv, device(x, y, z, 1 - c)).wait_recv()

    def signal(target):
        pl.semaphore_signal(barrier, inc=1, device_id=target, device_id_type=MESH)

    l_self = (x == y) & (y == z)
    r_holder = c == x // 2
    r_self = (x == z) & r_holder
    low_edge = (z == 3) & (c == 1)
    high_edge = (z == 0) & (c == 0)

    barrier = pltpu.get_barrier_semaphore()
    for d in range(1, 8):
        other = lax.rem(q + d, 8)
        signal((x, y * 8 + other))
    for d in range(1, 16):
        other = lax.rem(x * 4 + y + d, 16)
        signal((other // 4, lax.rem(other, 4) * 8 + q))

    @pl.when(jnp.logical_not(l_self))
    def _():
        signal(device(z, x, y, c))

    for k in range(2):
        @pl.when(r_holder & jnp.logical_not((x == z) & (c == k)))
        def _(k=k):
            signal(device(z, y, x, k))

    @pl.when(x != y)
    def _():
        signal(device(y, x, z, 1 - c))

    @pl.when(z == 3)
    def _():
        signal(device(y, turn(x, -1), 3, 1))

    @pl.when(z == 0)
    def _():
        signal(device(y, turn(x, 1), 0, 0))

    @pl.when(c == 0)
    def _():
        signal(device(x, turn(y, -1), z, 1))

    @pl.when(c == 1)
    def _():
        signal(device(x, turn(y, 1), z, 0))

    expected = (
        23
        + as_int(jnp.logical_not(l_self))
        + as_int(jnp.logical_not((x == z) & (c == z // 2)))
        + as_int(x != y)
        + 2 * as_int(low_edge | high_edge)
    )
    pl.semaphore_wait(barrier, expected)

    def psi_rows(first):
        return psi_in.at[pl.ds(pl.multiple_of(first, 128), 128)]

    def psi_columns(k):
        return psi.at[:, pl.ds(pl.multiple_of(x * 1024 + k * 512, 512), 512)]

    own_rows = 128 + z * 256 + c * 128
    for k in range(2):
        here = (x == y) & (c == k)

        @pl.when(here)
        def _(k=k):
            pltpu.make_async_copy(psi_columns(k), psi_rows(own_rows), psi1_r.at[c]).start()

        @pl.when(jnp.logical_not(here))
        def _(k=k):
            remote(
                psi_columns(k), psi_rows(own_rows), psi1_s.at[k], psi1_r.at[c],
                device(y, x, z, k),
            ).start()

        @pl.when(low_edge)
        def _(k=k):
            remote(
                psi_columns(k), psi_rows(0), psi1_s.at[2 + k], psi1_r.at[2],
                device(turn(y, 1), x, 3, k),
            ).start()

        @pl.when(high_edge)
        def _(k=k):
            remote(
                psi_columns(k), psi_rows(1152), psi1_s.at[2 + k], psi1_r.at[2],
                device(turn(y, -1), x, 0, k),
            ).start()

    pack(rband, r_out, rsec, bond * 2, None)
    r_slot = r_in.at[lax.rem(z, 2) * 2 + c]

    @pl.when((x == z) & (c == z // 2))
    def _():
        pltpu.make_async_copy(r_out, r_slot, r1_r.at[c]).start()

    @pl.when(jnp.logical_not((x == z) & (c == z // 2)))
    def _():
        remote(r_out, r_slot, r1_s.at[0], r1_r.at[c], device(z, y, x, z // 2)).start()

    pack(lband, l_out, lsec, bond * 2, terms)
    l_slot = l_in.at[z * 2 + c]

    @pl.when(l_self)
    def _():
        pltpu.make_async_copy(l_out, l_slot, l_r.at[0]).start()

    @pl.when(jnp.logical_not(l_self))
    def _():
        remote(l_out, l_slot, l1_s.at[0], l_r.at[0], device(y, z, x, c)).start()

    for k in range(2):
        arrived(psi_rows(128 + z * 256 + k * 128), psi1_s.at[k], psi1_r.at[k])
    psi_block = psi_in.at[pl.ds(pl.multiple_of(128 + z * 256, 128), 256)]
    for d in range(1, 4):
        remote(
            psi_block, psi_block, psi2_s.at[d - 1], psi2_r.at[d - 1],
            device(x, y, turn(z, d), c),
        ).start()

    @pl.when(z == 3)
    def _():
        arrived(psi_rows(0), psi1_s.at[2], psi1_r.at[2])
        for d in range(1, 4):
            remote(
                psi_rows(0), psi_rows(0), psi2_s.at[2 + d], psi2_r.at[3],
                device(x, y, turn(z, d), c),
            ).start()

    @pl.when(z == 0)
    def _():
        arrived(psi_rows(1152), psi1_s.at[2], psi1_r.at[2])
        for d in range(1, 4):
            remote(
                psi_rows(1152), psi_rows(1152), psi2_s.at[2 + d], psi2_r.at[4],
                device(x, y, turn(z, d), c),
            ).start()

    r_first = lax.rem(x, 2) * 2
    r_pair = r_in.at[pl.ds(r_first, 2)]

    @pl.when(r_holder)
    def _():
        for k in range(2):
            arrived(r_in.at[r_first + k], r1_s.at[0], r1_r.at[k])
        for d in range(1, 4):
            remote(
                r_pair, r_pair, r2_s.at[d - 1], r2_r.at[lax.rem(x, 2)],
                device(turn(x, d), y, z, c),
            ).start()

    l_mine = l_in.at[y * 2 + c]
    arrived(l_mine, l1_s.at[0], l_r.at[0])
    for d in range(1, 4):
        remote(
            l_mine, l_mine, l2_s.at[d - 1], l_r.at[d], device(x, turn(y, d), z, c)
        ).start()

    mine[...] = jnp.zeros_like(mine)
    out[...] = jnp.zeros_like(out)
    gram_at = {}
    row = 5
    for k in range(4):
        for m in range(k, 4):
            gram_at[k, m] = row
            row += 1

    def gram(i, held):
        at = pl.ds(pl.multiple_of(i * 64, 64), 64)
        vectors = [sub[k, at, :].astype(jnp.float32) for k in range(4)]
        new = []
        for k in range(4):
            for m in range(k, 4):
                new.append(
                    held[len(new)]
                    + jnp.sum((vectors[k] * vectors[m]).reshape(8, 8, 128), axis=0)
                )
        return tuple(new)

    held = lax.fori_loop(
        0, 16, gram, tuple(jnp.zeros((8, 128), jnp.float32) for _ in range(10))
    )
    for k in range(10):
        mine[5 + k : 6 + k, :] = jnp.sum(held[k], axis=0, keepdims=True)

    for d in range(1, 4):
        other = turn(z, -d)
        block = psi_in.at[pl.ds(pl.multiple_of(128 + other * 256, 128), 256)]
        arrived(block, psi2_s.at[0], psi2_r.at[d - 1])

    @pl.when(z != 3)
    def _():
        arrived(psi_rows(0), psi2_s.at[0], psi2_r.at[3])

    @pl.when(z != 0)
    def _():
        arrived(psi_rows(1152), psi2_s.at[0], psi2_r.at[4])

    def left_shard(group, core):
        base = group * 4 + core * 2
        for h in range(2):
            p = place_in_sector(lsec, x * 16 + base + h)
            weights = [as_int(p == at).astype(jnp.float32) for at in range(SEC_MOST)]
            bands = l_in[group * 2 + core, :, :, h * PACKED : (h + 1) * PACKED].reshape(DEEP, PACKED)
            for n in range(2):
                source = 0.0
                for at in range(SEC_MOST):
                    first = pl.multiple_of((base + 2 + h - at) * TILE, TILE)
                    weight = jnp.zeros((1, 256), jnp.float32) + weights[at]
                    source = source + psi_in[
                        pl.ds(first, PACKED), n * 256 : (n + 1) * 256
                    ] * weight.astype(jnp.bfloat16)
                made = jnp.dot(bands, source, preferred_element_type=jnp.float32).astype(
                    jnp.bfloat16
                )
                rows = pl.ds(pl.multiple_of((base + h) * TILE, TILE), TILE)
                for w in range(TERMS):
                    mid[w, rows, n * 256 : (n + 1) * 256] = made[w * TILE : (w + 1) * TILE]

    def left_step(k, carry):
        d = k + k // 2 - 2 * (k // 3)
        group = turn(y, -d)
        own = l_in.at[group * 2 + c]
        twin = l_in.at[group * 2 + 1 - c]

        @pl.when(k > 0)
        def _():
            arrived(own, l1_s.at[0], l_r.at[d])

        remote(own, own, lt_s.at[d], lt_r.at[d], device(x, y, z, 1 - c)).start()
        left_shard(group, c)
        arrived(twin, l1_s.at[0], lt_r.at[d])
        left_shard(group, 1 - c)
        return carry

    lax.fori_loop(0, 4, left_step, 0)

    for k in range(2):
        @pl.when(x != 2 * c + k)
        def _(k=k):
            arrived(r_in.at[2 * k : 2 * k + 2], r2_s.at[0], r2_r.at[k])

    gap = jnp.zeros((DEEP, TILE), jnp.bfloat16)
    low = []
    for b in range(4):
        for h in range(2):
            p = place_in_sector(rsec, y * 16 + c * 8 + b * 2 + h)
            rows = r_in[b, :, :, h * PACKED : (h + 1) * PACKED].reshape(DEEP, PACKED)
            near = jnp.concatenate([rows, gap], axis=1)
            far = jnp.concatenate([gap, rows], axis=1)
            shifted = as_int((p == 1) if h == 0 else (p != 1))
            chosen = (jnp.zeros((1, 256), jnp.int32) + shifted).astype(jnp.bfloat16)
            r_ready[2 * b + h] = far * chosen + near * (1.0 - chosen)
            low.append(as_int((p >= 1) if h == 0 else (p == 2)).astype(jnp.float32))

    def right_block(g, b):
        rows = pl.ds(pl.multiple_of(g * 256, 256), 256)
        parts = [0.0, 0.0, 0.0]
        for h in range(2):
            j = 2 * b + h
            left = jnp.concatenate(
                [mid[w, rows, j * TILE : (j + 1) * TILE] for w in range(TERMS)], axis=1
            )
            made = jnp.dot(left, r_ready[j], preferred_element_type=jnp.float32)
            first, second = made[:, :128], made[:, 128:]
            parts[0] = parts[0] + low[j] * first
            parts[1] = parts[1] + (low[j] * second + (1.0 - low[j]) * first)
            parts[2] = parts[2] + (1.0 - low[j]) * second
        for i in range(3):
            out[rows, (b + i) * 128 : (b + i + 1) * 128] += parts[i]

    left_next = device(x, turn(y, -1 * as_int(c == 0)), z, 1 - c)
    right_next = device(x, turn(y, as_int(c == 1)), z, 1 - c)

    def outer_step(g, carry):
        rows = pl.ds(pl.multiple_of(g * 256, 256), 256)
        right_block(g, 0)
        right_block(g, 3)
        remote(
            out.at[rows, 0:128], halo_in.at[1, rows], halo_s.at[g], halo_r.at[4 + g], left_next
        ).start()
        remote(
            out.at[rows, 640:768], halo_in.at[0, rows], halo_s.at[4 + g], halo_r.at[g], right_next
        ).start()
        return carry

    lax.fori_loop(0, 4, outer_step, 0)

    def inner_step(g, carry):
        rows = pl.ds(pl.multiple_of(g * 256, 256), 256)
        right_block(g, 1)
        right_block(g, 2)
        for side in range(2):
            arrived(halo_in.at[side, rows], halo_s.at[0], halo_r.at[4 * side + g])
        for b in range(4):
            total = out[rows, (b + 1) * 128 : (b + 2) * 128]
            if b == 0:
                total = total + halo_in[0, rows]
            if b == 3:
                total = total + halo_in[1, rows]
            zt, ct = 2 * c + b // 2, b % 2
            here = (z == zt) & (c == ct)

            @pl.when(here)
            def _(total=total):
                rs_in[z, rows] = total.astype(jnp.bfloat16)

            @pl.when(jnp.logical_not(here))
            def _(total=total, b=b, zt=zt, ct=ct):
                rs_out[b, rows] = total.astype(jnp.bfloat16)
                remote(
                    rs_out.at[b, rows], rs_in.at[z, rows], rs_s.at[b * 4 + g], rs_r.at[z * 4 + g],
                    device(x, y, zt, ct),
                ).start()
        return carry

    lax.fori_loop(0, 4, inner_step, 0)

    def sums(i, held):
        rows = pl.ds(pl.multiple_of(i * 256, 256), 256)
        for zs in range(4):
            @pl.when(jnp.logical_not((z == zs) & (c == z // 2)))
            def _(zs=zs):
                arrived(rs_in.at[zs, rows], rs_s.at[0], rs_r.at[zs * 4 + i])
        block = (rs_in[0, rows].astype(jnp.float32) + rs_in[1, rows].astype(jnp.float32)) + (
            rs_in[2, rows].astype(jnp.float32) + rs_in[3, rows].astype(jnp.float32)
        )
        app[rows] = block
        new = [held[0] + jnp.sum((block * block).reshape(32, 8, 128), axis=0)]
        for k in range(4):
            product = sub[k, rows, :].astype(jnp.float32) * block
            new.append(held[k + 1] + jnp.sum(product.reshape(32, 8, 128), axis=0))
        return tuple(new)

    held = lax.fori_loop(0, 4, sums, tuple(jnp.zeros((8, 128), jnp.float32) for _ in range(5)))
    for k in range(5):
        mine[k : k + 1, :] = jnp.sum(held[k], axis=0, keepdims=True)

    copies = []
    for d in range(1, 8):
        copy = remote(
            mine, first_in.at[d - 1], send_c.at[d - 1], recv_c.at[d - 1],
            (x, y * 8 + lax.rem(q + d, 8)),
        )
        copy.start()
        copies.append(copy)
    for copy in copies:
        copy.wait()
    added = mine[...]
    for d in range(7):
        added = added + first_in[d]
    second_out[...] = added
    copies = []
    for d in range(1, 16):
        other = lax.rem(x * 4 + y + d, 16)
        copy = remote(
            second_out, second_in.at[d - 1], send_d.at[d - 1], recv_d.at[d - 1],
            (other // 4, lax.rem(other, 4) * 8 + q),
        )
        copy.start()
        copies.append(copy)
    for copy in copies:
        copy.wait()
    for d in range(15):
        added = added + second_in[d]
    sums_all = jnp.sum(added, axis=1, keepdims=True)

    def one(i):
        return sums_all[i : i + 1, :] * (1.0 / float(D_LEFT * D_RIGHT))

    coefficient = [one(1 + k) / (one(gram_at[k, k]) + epsilon) for k in range(4)]
    energy = one(0)
    for k in range(4):
        energy = energy - 2.0 * coefficient[k] * one(1 + k)
        for m in range(k, 4):
            twice = 1.0 if m == k else 2.0
            energy = energy + twice * coefficient[k] * coefficient[m] * one(gram_at[k, m])
    scale = lax.rsqrt(jnp.maximum(energy, 0.0) + epsilon)

    def write(i, carry):
        rows = pl.ds(pl.multiple_of(i * 128, 128), 128)
        block = app[rows]
        residual = block
        for k in range(4):
            residual = residual - coefficient[k] * sub[k, rows, :].astype(jnp.float32)
        applied_ref[rows, :] = block
        vector_ref[rows, :] = residual * scale
        return carry

    lax.fori_loop(0, 8, write, 0)

    def left(src, send):
        remote(src, src, send, l_r.at[0], device(x, y, z, 1 - c)).wait_send()

    for k in range(2):
        @pl.when(jnp.logical_not((x == y) & (c == k)))
        def _(k=k):
            left(psi_columns(k), psi1_s.at[k])

        @pl.when(low_edge | high_edge)
        def _(k=k):
            left(psi_columns(k), psi1_s.at[2 + k])

    @pl.when(jnp.logical_not((x == z) & (c == z // 2)))
    def _():
        left(r_out, r1_s.at[0])

    @pl.when(jnp.logical_not(l_self))
    def _():
        left(l_out, l1_s.at[0])

    for d in range(1, 4):
        left(psi_block, psi2_s.at[d - 1])
        left(l_mine, l2_s.at[d - 1])

        @pl.when((z == 3) | (z == 0))
        def _(d=d):
            left(psi_rows(0), psi2_s.at[2 + d])

        @pl.when(r_holder)
        def _(d=d):
            left(r_pair, r2_s.at[d - 1])

    for g in range(4):
        left(l_mine, lt_s.at[g])
        rows = slice(g * 256, (g + 1) * 256)
        left(out.at[rows, 0:128], halo_s.at[g])
        left(out.at[rows, 640:768], halo_s.at[4 + g])
        for b in range(4):
            zt, ct = 2 * c + b // 2, b % 2

            @pl.when(jnp.logical_not((z == zt) & (c == ct)))
            def _(b=b, rows=rows, g=g):
                left(rs_out.at[b, rows], rs_s.at[b * 4 + g])


def per_device(
    wavefunction, subspace, left_band, right_band, left_sector, right_sector, term_sectors
):
    shape = jax.ShapeDtypeStruct((1024, 128), jnp.float32)
    dma = pltpu.SemaphoreType.DMA
    bf16, f32 = jnp.bfloat16, jnp.float32
    vmem = pl.BlockSpec(memory_space=pltpu.VMEM)
    smem = pl.BlockSpec(memory_space=pltpu.SMEM)
    shard = (TERMS, TILE, 2 * PACKED)
    return pl.pallas_call(
        kernel,
        out_shape=(shape, shape),
        in_specs=[smem, smem, vmem, vmem, vmem, vmem, vmem],
        out_specs=(vmem, vmem),
        scratch_shapes=[
            pltpu.VMEM(shard, bf16),
            pltpu.VMEM(shard, bf16),
            pltpu.VMEM((8,) + shard, bf16),
            pltpu.VMEM((4,) + shard, bf16),
            pltpu.VMEM((1280, 512), bf16),
            pltpu.VMEM((8, DEEP, 256), bf16),
            pltpu.VMEM((TERMS, 1024, 512), bf16),
            pltpu.VMEM((1024, 768), f32),
            pltpu.VMEM((2, 1024, 128), f32),
            pltpu.VMEM((4, 1024, 128), bf16),
            pltpu.VMEM((4, 1024, 128), bf16),
            pltpu.VMEM((1024, 128), f32),
            pltpu.VMEM((16, 128), f32),
            pltpu.VMEM((7, 16, 128), f32),
            pltpu.VMEM((16, 128), f32),
            pltpu.VMEM((15, 16, 128), f32),
            dma((4,)), dma((3,)), dma((6,)), dma((5,)),
            dma((1,)), dma((2,)), dma((3,)), dma((2,)),
            dma((1,)), dma((3,)), dma((4,)), dma((4,)), dma((4,)),
            dma((8,)), dma((8,)), dma((16,)), dma((16,)),
            dma((7,)), dma((7,)), dma((15,)), dma((15,)),
        ],
        compiler_params=pltpu.CompilerParams(
            collective_id=0, has_side_effects=True, vmem_limit_bytes=56 * 1024 * 1024
        ),
        name="two_site_step",
    )(left_sector, right_sector, term_sectors, wavefunction, subspace, left_band, right_band)


def solution(mesh):
    return jax.shard_map(
        per_device,
        mesh=mesh,
        in_specs=(
            P("bond", None),
            P(None, "mpo", "bond"),
            P("mpo", "bond", None),
            P("mpo", "bond", None),
            P(),
            P(),
            P("mpo", None),
        ),
        out_specs=(P("mpo", "bond"), P("mpo", "bond")),
        check_vma=False,
    )
```

time: 428 us -> 132 us (0.31)
  waiting for transfers between devices: 144 us -> 0 us
  blocking collectives: 129 us -> 0 us
  Pallas kernels: 0 us -> 125 us
  local copies, waits for them, and re-layouts: 68.9 us -> 6.56 us
  matrix products: 36.4 us -> 0 us
  other arithmetic: 17.7 us -> 0 us
  starting transfers between devices: 15.2 us -> 0 us
  between operations: 15 us -> 0.66 us
    psum x2 -> x0, blocking collectives: 129 us -> none  [the longest x1 64.9 us: per_device(): lax.psum((local_correlation, local_square), ('mpo', 'bond'))]
    pallas_call x0 -> x1, Pallas kernels: none -> 125 us  [per_device(): pl.pallas_call(kernel, out_shape=(shape, shape), in_specs=[smem, smem, vm...]
    all_gather x1 -> x0, waiting for transfers between devices: 68.2 us -> none  [per_device(): all_bands = lax.all_gather(left_band, 'bond', axis=1, tiled=True)]
    convert_element_type x3 -> x0, local copies, waits for them, and re-layouts: 51.8 us -> none  [the longest x2 51.7 us: left_section(): running.reshape(groups, tile_count * TILE, columns).astype(jnp.bfloat16)]
    dot_general x4 -> x0, matrix products: 36.4 us -> none  [the longest x1 17.8 us: left_section(): jnp.einsum('wtib,tbc->wtic', blocks, stacked, preferred_element_type=jnp....]
    reduce_scatter x1 -> x0, waiting for transfers between devices: 31.2 us -> none  [per_device(): applied = lax.psum_scatter(centre, 'mpo', scatter_dimension=0, tiled=True)]
    ppermute x2 -> x0, waiting for transfers between devices: 23 us -> none  [the longest x1 21.8 us: extended(): lax.ppermute(head, axis, [((i + 1) % count, i) for i in range(ends)])]
    all_to_all x1 -> x0, waiting for transfers between devices: 22.1 us -> none  [per_device(): lax.all_to_all(wavefunction, 'bond', split_axis=1, concat_axis=0, tiled=T...]
  transfers between devices with their start and end apart: 5 -> 0, of which waited for: 5 -> 0; matrix products, arithmetic and copies ran while one was open for 3% -> 0% of each run, Pallas kernels for 0% -> 0%
where the time goes in v2:
time: 132 us
  Pallas kernels  125 us (95%)
  local copies, waits for them, and re-layouts  6.56 us (5%)
    pallas_call x1, Pallas kernels, per_device(): pl.pallas_call(kernel, out_shape=(shape, shape), in_specs=[smem, smem, vm...  125 us
    unnamed x8, local copies, waits for them, and re-layouts  6.56 us

profile of v2, /device:TPU:1, one launch (start us, length us, event | category | flops | bytes accessed | tf_op | source)
XLA Modules:
  0.0 132.0 jit_solution(11997613913732349232)
XLA Ops:
  0.6 0.0 copy-start
  0.6 2.3 %copy.9.lband = bf16[9,128,320]{2,1,0:T(8,128)(2,1)} copy(bf16[9,128,320]{1,2,0:T(8,128)(2,1)} %param.9) | data formatting | bytes 1474560 | tf_op args[2]
  2.9 0.0 copy-done
  2.9 1.6 %copy.10.rband = bf16[9,128,320]{2,1,0:T(8,128)(2,1)} copy(bf16[9,128,320]{1,2,0:T(8,128)(2,1)S(1)} %copy-done) | data formatting | bytes 1474560 | tf_op args[3]
  4.5 124.8 %two_site_step.1 = (f32[1024,128]{1,0:T(8,128)}, f32[1024,128]{1,0:T(8,128)}) custom-call(s32[64]{0:T(128)} %lsec.1, s32[64]{0:T(128)} %rsec.1, s32[9,32]{1,0:T(8,128)} %terms.1, bf16[128,4096]{1,0:T(8,128)(2,1)} %psi.1, bf16[4,1024,128]{2,1,0:T(8,128)(2,1)} %sub.1, bf16[9,128,320]{2,1,0:T(8,128)(2,1)} %copy.9.lband, bf16[9,128,320]{2,1,0:T(8,128)(2,1)} %copy.10.rband), custom_call_target="tpu_custom_call" | custom-call | tf_op jit(solution)/shard_map/two_site_step/pallas_call | solution.py:546
  129.3 0.0 copy-start.1
  129.3 1.9 %copy.13 = f32[1024,128]{1,0:T(8,128)} copy(f32[1024,128]{1,0:T(8,128)} %get-tuple-element.4) | data formatting | bytes 1048576
  131.3 0.0 copy-done.1
  131.3 0.8 copy.14
Async XLA Ops:
  0.6 2.3 %copy-start = (bf16[9,128,320]{1,2,0:T(8,128)(2,1)S(1)}, bf16[9,128,320]{1,2,0:T(8,128)(2,1)}, u32[]{:S(2)}) copy-start(bf16[9,128,320]{1,2,0:T(8,128)(2,1)} %param.10) | copy-start | bytes 2211844
  129.3 1.9 %copy-start.1 = (f32[1024,128]{1,0:T(8,128)S(1)}, f32[1024,128]{1,0:T(8,128)}, u32[]{:S(2)}) copy-start(f32[1024,128]{1,0:T(8,128)} %get-tuple-element.5) | copy-start | bytes 1572868

commit v3 on v2

v3 whole, which is shorter than its diff:
```python
import functools

import jax
import jax.numpy as jnp
from jax import lax
from jax.experimental import pallas as pl
from jax.experimental.pallas import tpu as pltpu
from jax.sharding import PartitionSpec as P

D_LEFT = 4096
D_RIGHT = 4096
TILE = 64
SEC_MOST = 3
PACKED = SEC_MOST * TILE
NT = 64
TERMS = 9
DEEP = TERMS * TILE
MESH = pl.DeviceIdType.MESH

epsilon = 1e-06


def as_int(flag):
    return flag.astype(jnp.int32)


def place_in_sector(sector, tile):
    here = sector[tile]
    one = as_int((tile >= 1) & (sector[jnp.maximum(tile - 1, 0)] == here))
    two = as_int((tile >= 2) & (sector[jnp.maximum(tile - 2, 0)] == here))
    return one + two


def sector_size(sector, tile):
    here = sector[tile]
    one = as_int((tile <= NT - 2) & (sector[jnp.minimum(tile + 1, NT - 1)] == here))
    two = as_int((tile <= NT - 3) & (sector[jnp.minimum(tile + 2, NT - 1)] == here))
    return 1 + place_in_sector(sector, tile) + one + two


def lanes_of(low, high):
    half = lax.broadcasted_iota(jnp.int32, (1, 128), 1) // TILE
    return low * (1 - half) + high * half


def pack_masks(sector, first_tile):
    row = lax.broadcasted_iota(jnp.int32, (PACKED, 128), 0)
    place = [place_in_sector(sector, first_tile + h) for h in range(2)]
    size = [sector_size(sector, first_tile + h) * TILE for h in range(2)]
    return [
        jnp.clip(
            lanes_of(size[0] * as_int(place[0] == at), size[1] * as_int(place[1] == at)) - row, 0, 1
        ).astype(jnp.bfloat16)
        for at in range(SEC_MOST)
    ]


def packed_term(band, w, masks):
    total = band[w, 2 * TILE : 2 * TILE + PACKED, :] * masks[0]
    total = total + band[w, TILE : TILE + PACKED, :] * masks[1]
    return total + band[w, :PACKED, :] * masks[2]


def kernel(
    lsec, rsec, terms, psi, sub, lband, rband,
    applied_ref, vector_ref,
    l_in, r_out, r_in, psi_in, r_wide, mid, out, halo_in, rs_out, rs_in, deal, app,
    mine, first_in, second_out, second_in,
    psi1_s, psi1_r, psi2_s, psi2_r, r_s, r_r, l_s, l_r, lt_s, lt_r,
    halo_s, halo_r, rs_s, rs_r, deal_s, deal_r, send_c, recv_c, send_d, recv_d,
):
    x = lax.axis_index("mpo")
    bond = lax.axis_index("bond")
    y = bond // 8
    q = lax.rem(bond, 8)
    z = q // 2
    c = lax.rem(q, 2)

    def device(dx, dy, dz, dc):
        return (dx, dy * 8 + dz * 2 + dc)

    def turn(value, step):
        return lax.rem(value + step + 4, 4)

    def remote(src, dst, send, recv, target):
        return pltpu.make_async_remote_copy(
            src_ref=src, dst_ref=dst, send_sem=send, recv_sem=recv,
            device_id=target, device_id_type=MESH,
        )

    twin = device(x, y, z, 1 - c)

    def arrived(dst, recv):
        remote(dst, dst, l_s.at[0], recv, twin).wait_recv()

    def left(src, send):
        remote(src, src, send, l_r.at[0], twin).wait_send()

    def signal(target):
        pl.semaphore_signal(barrier, inc=1, device_id=target, device_id_type=MESH)

    barrier = pltpu.get_barrier_semaphore()
    for d in range(1, 8):
        signal((x, y * 8 + lax.rem(q + d, 8)))
    for d in range(1, 16):
        other = lax.rem(x * 4 + y + d, 16)
        signal((other // 4, lax.rem(other, 4) * 8 + q))
    for d in range(1, 4):
        signal(device(x, turn(y, d), z, 1 - c))
        signal(device(x, turn(y, d), turn(z, -1), 1))
        signal(device(x, turn(y, d), turn(z, 1), 0))
    pl.semaphore_wait(barrier, 31)

    above = as_int((z == 3) & (c == 1))
    below = as_int((z == 0) & (c == 0))
    halo_y = turn(y, above - below)
    halo_z = turn(z, 2 * c - 1)
    halo_slot = 3 * (1 - c)
    own_rows = pl.ds(pl.multiple_of(x * 32, 32), 32)

    def psi_part(dy, k):
        return psi.at[own_rows, pl.ds(pl.multiple_of(dy * 1024 + k * 512, 512), 512)]

    for d in range(4):
        dy = turn(y, d)
        for k in range(2):
            n = 2 * d + k
            own = psi_in.at[y, 1 + c, x]
            if d == 0:
                @pl.when(c == k)
                def _(k=k, own=own, dy=dy):
                    pltpu.make_async_copy(psi_part(dy, k), own, psi1_r.at[y * 4 + 1 + c]).start()

                @pl.when(c != k)
                def _(k=k, own=own, dy=dy, n=n):
                    remote(
                        psi_part(dy, k), own, psi1_s.at[n], psi1_r.at[y * 4 + 1 + c],
                        device(x, dy, z, k),
                    ).start()
            else:
                remote(
                    psi_part(dy, k), own, psi1_s.at[n], psi1_r.at[y * 4 + 1 + c],
                    device(x, dy, z, k),
                ).start()
            remote(
                psi_part(dy, k), psi_in.at[halo_y, halo_slot, x], psi1_s.at[8 + n],
                psi1_r.at[halo_y * 4 + halo_slot], device(x, dy, halo_z, k),
            ).start()

    masks = pack_masks(lsec, bond * 2)
    number = lax.broadcasted_iota(jnp.int32, terms.shape, 1)
    active = []
    for h in range(2):
        same = 1 - jnp.clip(jnp.abs(number - lsec[bond * 2 + h]), 0, 1)
        active.append(jnp.sum(terms[...] * same, axis=1, keepdims=True))
    l_mine = l_in.at[y * 2 + c]
    for w in range(TERMS):
        switch = lanes_of(active[0][w : w + 1], active[1][w : w + 1]).astype(jnp.bfloat16)
        rows = (packed_term(lband, w, masks) * switch).T
        l_in[y * 2 + c, w] = jnp.concatenate([rows[:TILE], rows[TILE:]], axis=1)
    for d in range(1, 4):
        remote(l_mine, l_mine, l_s.at[d - 1], l_r.at[d], device(x, turn(y, d), z, c)).start()

    masks = pack_masks(rsec, bond * 2)
    for w in range(TERMS):
        r_out[w] = packed_term(rband, w, masks)
    r_slot = lax.rem(z, 2) * 2 + c

    @pl.when(c == z // 2)
    def _():
        pltpu.make_async_copy(r_out, r_in.at[r_slot], r_r.at[r_slot]).start()

    @pl.when(c != z // 2)
    def _():
        remote(r_out, r_in.at[r_slot], r_s.at[0], r_r.at[r_slot], twin).start()

    for d in range(1, 4):
        remote(
            r_out, r_in.at[r_slot], r_s.at[d], r_r.at[r_slot], device(x, y, turn(z, d), z // 2)
        ).start()

    order = [0, 1, 3, 2]
    for k in range(4):
        group = turn(y, -order[k])
        for slot in range(4):
            arrived(psi_in.at[group, slot, x], psi1_r.at[group * 4 + slot])
        part = psi_in.at[group, :, x]
        for d in range(1, 4):
            remote(
                part, part, psi2_s.at[3 * k + d - 1], psi2_r.at[4 * (d - 1) + group],
                device(turn(x, d), y, z, c),
            ).start()

    mine[...] = jnp.zeros_like(mine)
    out[...] = jnp.zeros_like(out)
    gram_at = {}
    row = 5
    for k in range(4):
        for m in range(k, 4):
            gram_at[k, m] = row
            row += 1

    def gram(i, held):
        at = pl.ds(pl.multiple_of(i * 64, 64), 64)
        vectors = [sub[k, at, :].astype(jnp.float32) for k in range(4)]
        new = []
        for k in range(4):
            for m in range(k, 4):
                new.append(
                    held[len(new)]
                    + jnp.sum((vectors[k] * vectors[m]).reshape(8, 8, 128), axis=0)
                )
        return tuple(new)

    held = lax.fori_loop(
        0, 16, gram, tuple(jnp.zeros((8, 128), jnp.float32) for _ in range(10))
    )
    for k in range(10):
        mine[5 + k : 6 + k, :] = jnp.sum(held[k], axis=0, keepdims=True)

    def left_shard(group, core):
        for h in range(2):
            p = place_in_sector(lsec, group * 16 + z * 4 + core * 2 + h)
            weights = [
                (jnp.zeros((1, 256), jnp.int32) + as_int(p == at)).astype(jnp.bfloat16)
                for at in range(SEC_MOST)
            ]
            bands = l_in[group * 2 + core, :, :, h * PACKED : (h + 1) * PACKED].reshape(DEEP, PACKED)
            first = 2 + core * 2 + h
            rows = pl.ds(pl.multiple_of(group * 256 + core * 128 + h * TILE, TILE), TILE)
            for n in range(2):
                lanes = slice(n * 256, (n + 1) * 256)
                tiles = {
                    t: jnp.concatenate(
                        [psi_in[group, t // 2, (t % 2) * 2 + i, :, lanes] for i in range(2)], axis=0
                    )
                    for t in range(first - 2, first + 3)
                }
                source = jnp.concatenate(
                    [
                        tiles[first + m] * weights[0]
                        + tiles[first + m - 1] * weights[1]
                        + tiles[first + m - 2] * weights[2]
                        for m in range(SEC_MOST)
                    ],
                    axis=0,
                )
                made = jnp.dot(bands, source, preferred_element_type=jnp.float32).astype(
                    jnp.bfloat16
                )
                for w in range(TERMS):
                    mid[w, rows, lanes] = made[w * TILE : (w + 1) * TILE]

    def left_step(k, carry):
        d = k + k // 2 - 2 * (k // 3)
        group = turn(y, -d)
        own = l_in.at[group * 2 + c]

        @pl.when(k > 0)
        def _():
            arrived(own, l_r.at[d])

        remote(own, own, lt_s.at[d], lt_r.at[d], twin).start()
        for e in range(1, 4):
            arrived(psi_in.at[group, :, turn(x, -e)], psi2_r.at[4 * (e - 1) + group])
        arrived(l_in.at[group * 2 + 1 - c], lt_r.at[d])
        left_shard(group, 0)
        left_shard(group, 1)
        return carry

    lax.fori_loop(0, 4, left_step, 0)

    for b in range(4):
        arrived(r_in.at[b], r_r.at[b])
        place = [place_in_sector(rsec, y * 16 + c * 8 + b * 2 + h) for h in range(2)]
        weights = {}
        for i in range(6):
            for m in range(SEC_MOST):
                weights[i, m] = lanes_of(
                    as_int(place[0] == m - i + 2), as_int(place[1] == m - i + 3)
                ).astype(jnp.bfloat16)
        for w in range(TERMS):
            parts = [r_in[b, w, m * TILE : (m + 1) * TILE, :] for m in range(SEC_MOST)]
            for i in range(6):
                total = None
                for m in range(SEC_MOST):
                    if 0 <= m - i + 3 <= 3:
                        term = parts[m] * weights[i, m]
                        total = term if total is None else total + term
                r_wide[b, i * TILE : (i + 1) * TILE, w * 128 : (w + 1) * 128] = total

    def right_block(g, b):
        rows = pl.ds(pl.multiple_of(g * 256, 256), 256)
        source = jnp.concatenate(
            [mid[w, rows, b * 128 : (b + 1) * 128] for w in range(TERMS)], axis=1
        )
        out[rows, b * 128 : b * 128 + 384] += lax.dot_general(
            source, r_wide[b], (((1,), (1,)), ((), ())), preferred_element_type=jnp.float32
        )

    left_next = device(x, turn(y, -1 * as_int(c == 0)), z, 1 - c)
    right_next = device(x, turn(y, as_int(c == 1)), z, 1 - c)

    def outer_step(i, carry):
        g = turn(x, i + 1)
        rows = pl.ds(pl.multiple_of(g * 256, 256), 256)
        right_block(g, 0)
        right_block(g, 3)
        remote(
            out.at[rows, 0:128], halo_in.at[1, rows], halo_s.at[i], halo_r.at[4 + i], left_next
        ).start()
        remote(
            out.at[rows, 640:768], halo_in.at[0, rows], halo_s.at[4 + i], halo_r.at[i], right_next
        ).start()
        return carry

    lax.fori_loop(0, 4, outer_step, 0)

    def columns_done(i, g):
        rows = pl.ds(pl.multiple_of(g * 256, 256), 256)
        right_block(g, 1)
        right_block(g, 2)
        for side in range(2):
            arrived(halo_in.at[side, rows], halo_r.at[4 * side + i])
        return [
            out[rows, 128:256] + halo_in[0, rows],
            out[rows, 256:384],
            out[rows, 384:512],
            out[rows, 512:640] + halo_in[1, rows],
        ]

    def inner_step(i, carry):
        g = turn(x, i + 1)
        for b, total in enumerate(columns_done(i, g)):
            rs_out[i, :, b * 128 : (b + 1) * 128] = total.astype(jnp.bfloat16)
        remote(rs_out.at[i], rs_in.at[i], rs_s.at[i], rs_r.at[i], device(g, y, z, c)).start()
        return carry

    lax.fori_loop(0, 3, inner_step, 0)
    kept = columns_done(3, x)
    for i in range(3):
        arrived(rs_in.at[i], rs_r.at[i])
    place_rows = pl.ds(pl.multiple_of(z * 256, 256), 256)
    for b in range(4):
        lanes = slice(b * 128, (b + 1) * 128)
        total = kept[b]
        for i in range(3):
            total = total + rs_in[i, :, lanes].astype(jnp.float32)
        zt, ct = 2 * c + b // 2, b % 2
        here = (z == zt) & (c == ct)

        @pl.when(here)
        def _(total=total):
            app[place_rows] = total

        @pl.when(jnp.logical_not(here))
        def _(total=total, b=b, zt=zt, ct=ct):
            deal[b] = total
            remote(
                deal.at[b], app.at[place_rows], deal_s.at[b], deal_r.at[z], device(x, y, zt, ct)
            ).start()

    def sums(i, held):
        rows = pl.ds(pl.multiple_of(i * 256, 256), 256)

        @pl.when(jnp.logical_not((z == i) & (c == z // 2)))
        def _():
            arrived(app.at[rows], deal_r.at[i])

        block = app[rows]
        new = [held[0] + jnp.sum((block * block).reshape(32, 8, 128), axis=0)]
        for k in range(4):
            product = sub[k, rows, :].astype(jnp.float32) * block
            new.append(held[k + 1] + jnp.sum(product.reshape(32, 8, 128), axis=0))
        return tuple(new)

    held = lax.fori_loop(0, 4, sums, tuple(jnp.zeros((8, 128), jnp.float32) for _ in range(5)))
    for k in range(5):
        mine[k : k + 1, :] = jnp.sum(held[k], axis=0, keepdims=True)

    copies = []
    for d in range(1, 8):
        copy = remote(
            mine, first_in.at[d - 1], send_c.at[d - 1], recv_c.at[d - 1],
            (x, y * 8 + lax.rem(q + d, 8)),
        )
        copy.start()
        copies.append(copy)
    for copy in copies:
        copy.wait()
    added = mine[...]
    for d in range(7):
        added = added + first_in[d]
    second_out[...] = added
    copies = []
    for d in range(1, 16):
        other = lax.rem(x * 4 + y + d, 16)
        copy = remote(
            second_out, second_in.at[d - 1], send_d.at[d - 1], recv_d.at[d - 1],
            (other // 4, lax.rem(other, 4) * 8 + q),
        )
        copy.start()
        copies.append(copy)
    for copy in copies:
        copy.wait()
    for d in range(15):
        added = added + second_in[d]
    sums_all = jnp.sum(added, axis=1, keepdims=True)

    def one(i):
        return sums_all[i : i + 1, :] * (1.0 / float(D_LEFT * D_RIGHT))

    coefficient = [one(1 + k) / (one(gram_at[k, k]) + epsilon) for k in range(4)]
    energy = one(0)
    for k in range(4):
        energy = energy - 2.0 * coefficient[k] * one(1 + k)
        for m in range(k, 4):
            twice = 1.0 if m == k else 2.0
            energy = energy + twice * coefficient[k] * coefficient[m] * one(gram_at[k, m])
    scale = lax.rsqrt(jnp.maximum(energy, 0.0) + epsilon)

    def write(i, carry):
        rows = pl.ds(pl.multiple_of(i * 128, 128), 128)
        block = app[rows]
        residual = block
        for k in range(4):
            residual = residual - coefficient[k] * sub[k, rows, :].astype(jnp.float32)
        applied_ref[rows, :] = block
        vector_ref[rows, :] = residual * scale
        return carry

    lax.fori_loop(0, 8, write, 0)

    for n in range(8):
        if n < 2:
            @pl.when(c != n)
            def _(n=n):
                left(psi_part(y, n), psi1_s.at[n])
        else:
            left(psi_part(y, 0), psi1_s.at[n])
        left(psi_part(y, 0), psi1_s.at[8 + n])

    @pl.when(c != z // 2)
    def _():
        left(r_out, r_s.at[0])

    for d in range(1, 4):
        left(r_out, r_s.at[d])
        left(l_mine, l_s.at[d - 1])
        left(rs_out.at[d - 1], rs_s.at[d - 1])
    for n in range(12):
        left(psi_in.at[0, :, x], psi2_s.at[n])
    for g in range(4):
        left(l_mine, lt_s.at[g])
        left(out.at[0:256, 0:128], halo_s.at[g])
        left(out.at[0:256, 640:768], halo_s.at[4 + g])
        zt, ct = 2 * c + g // 2, g % 2

        @pl.when(jnp.logical_not((z == zt) & (c == ct)))
        def _(g=g):
            left(deal.at[g], deal_s.at[g])


def per_device(
    wavefunction, subspace, left_band, right_band, left_sector, right_sector, term_sectors
):
    shape = jax.ShapeDtypeStruct((1024, 128), jnp.float32)
    dma = pltpu.SemaphoreType.DMA
    bf16, f32 = jnp.bfloat16, jnp.float32
    vmem = pl.BlockSpec(memory_space=pltpu.VMEM)
    smem = pl.BlockSpec(memory_space=pltpu.SMEM)
    return pl.pallas_call(
        kernel,
        out_shape=(shape, shape),
        in_specs=[smem, smem, vmem, vmem, vmem, vmem, vmem],
        out_specs=(vmem, vmem),
        scratch_shapes=[
            pltpu.VMEM((8, TERMS, TILE, 2 * PACKED), bf16),
            pltpu.VMEM((TERMS, PACKED, 128), bf16),
            pltpu.VMEM((4, TERMS, PACKED, 128), bf16),
            pltpu.VMEM((4, 4, 4, 32, 512), bf16),
            pltpu.VMEM((4, 384, TERMS * 128), bf16),
            pltpu.VMEM((TERMS, 1024, 512), bf16),
            pltpu.VMEM((1024, 768), f32),
            pltpu.VMEM((2, 1024, 128), f32),
            pltpu.VMEM((3, 256, 512), bf16),
            pltpu.VMEM((3, 256, 512), bf16),
            pltpu.VMEM((4, 256, 128), f32),
            pltpu.VMEM((1024, 128), f32),
            pltpu.VMEM((16, 128), f32),
            pltpu.VMEM((7, 16, 128), f32),
            pltpu.VMEM((16, 128), f32),
            pltpu.VMEM((15, 16, 128), f32),
            dma((16,)), dma((16,)), dma((12,)), dma((12,)),
            dma((4,)), dma((4,)), dma((3,)), dma((4,)), dma((4,)), dma((4,)),
            dma((8,)), dma((8,)), dma((3,)), dma((3,)), dma((4,)), dma((4,)),
            dma((7,)), dma((7,)), dma((15,)), dma((15,)),
        ],
        compiler_params=pltpu.CompilerParams(
            collective_id=0, has_side_effects=True, vmem_limit_bytes=56 * 1024 * 1024
        ),
        name="two_site_step",
    )(
        left_sector, right_sector, term_sectors, wavefunction, subspace,
        jnp.swapaxes(left_band, 1, 2), jnp.swapaxes(right_band, 1, 2),
    )


def solution(mesh):
    return jax.shard_map(
        per_device,
        mesh=mesh,
        in_specs=(
            P("bond", None),
            P(None, "mpo", "bond"),
            P("mpo", "bond", None),
            P("mpo", "bond", None),
            P(),
            P(),
            P("mpo", None),
        ),
        out_specs=(P("mpo", "bond"), P("mpo", "bond")),
        check_vma=False,
    )
```

time: 132 us -> 89.5 us (0.68)
  Pallas kernels: 125 us -> 85.9 us
  local copies, waits for them, and re-layouts: 6.56 us -> 2.72 us
    pallas_call x1, Pallas kernels: 125 us -> 85.9 us  [per_device(): pl.pallas_call(kernel, out_shape=(shape, shape), in_specs=[smem, smem, vm...]
    unnamed x8 -> x4, local copies, waits for them, and re-layouts: 6.56 us -> 2.72 us
where the time goes in v3:
time: 89.5 us; the launch traced here: 89.3 us
  Pallas kernels  85.9 us (96%)
  local copies, waits for them, and re-layouts  2.72 us (3%)
    pallas_call x1, Pallas kernels, per_device(): pl.pallas_call(kernel, out_shape=(shape, shape), in_specs=[smem, smem, vm...  85.9 us
    unnamed x4, local copies, waits for them, and re-layouts  2.72 us

profile of v3, /device:TPU:1, one launch (start us, length us, event | category | flops | bytes accessed | tf_op | source)
XLA Modules:
  0.0 89.3 jit_solution(15929239821407516381)
XLA Ops:
  0.6 85.9 %two_site_step.1 = (f32[1024,128]{1,0:T(8,128)}, f32[1024,128]{1,0:T(8,128)}) custom-call(s32[64]{0:T(128)} %lsec.1, s32[64]{0:T(128)} %rsec.1, s32[9,32]{1,0:T(8,128)} %terms.1, bf16[128,4096]{1,0:T(8,128)(2,1)} %psi.1, bf16[4,1024,128]{2,1,0:T(8,128)(2,1)} %sub.1, bf16[9,320,128]{2,1,0:T(8,128)(2,1)} %bitcast.2, bf16[9,320,128]{2,1,0:T(8,128)(2,1)} %bitcast.3), custom_call_target="tpu_custom_call" | custom-call | tf_op jit(solution)/shard_map/two_site_step/pallas_call | solution.py:472
  86.6 0.0 copy-start
  86.6 1.9 %copy.11 = f32[1024,128]{1,0:T(8,128)} copy(f32[1024,128]{1,0:T(8,128)} %get-tuple-element.4) | data formatting | bytes 1048576
  88.5 0.0 copy-done
  88.5 0.8 copy.12
Async XLA Ops:
  86.6 1.9 %copy-start = (f32[1024,128]{1,0:T(8,128)S(1)}, f32[1024,128]{1,0:T(8,128)}, u32[]{:S(2)}) copy-start(f32[1024,128]{1,0:T(8,128)} %get-tuple-element.5) | copy-start | bytes 1572868

commit v4 on v3

--- a/solution.py
+++ b/solution.py
@@ -64,10 +64,10 @@
 def kernel(
     lsec, rsec, terms, psi, sub, lband, rband,
     applied_ref, vector_ref,
-    l_in, r_out, r_in, psi_in, r_wide, mid, out, halo_in, rs_out, rs_in, deal, app,
+    l_in, r_out, r_in, psi_in, r_wide, mid, out, halo_out, halo_in, rs_out, rs_in, sub_in, deal, app,
     mine, first_in, second_out, second_in,
-    psi1_s, psi1_r, psi2_s, psi2_r, r_s, r_r, l_s, l_r, lt_s, lt_r,
-    halo_s, halo_r, rs_s, rs_r, deal_s, deal_r, send_c, recv_c, send_d, recv_d,
+    psi1_s, psi1_r, psi2_s, psi2_r, r_s, r_r, rf_r, l_s, l_r, lt_s, lt_r,
+    halo_s, halo_r, rs_s, rs_r, sub_s, sub_r, deal_s, deal_r, send_c, recv_c, send_d, recv_d,
 ):
     x = lax.axis_index("mpo")
     bond = lax.axis_index("bond")
@@ -109,6 +109,22 @@
         signal(device(x, turn(y, d), z, 1 - c))
         signal(device(x, turn(y, d), turn(z, -1), 1))
         signal(device(x, turn(y, d), turn(z, 1), 0))
+    masks = pack_masks(lsec, bond * 2)
+    number = lax.broadcasted_iota(jnp.int32, terms.shape, 1)
+    active = []
+    for h in range(2):
+        same = 1 - jnp.clip(jnp.abs(number - lsec[bond * 2 + h]), 0, 1)
+        active.append(jnp.sum(terms[...] * same, axis=1, keepdims=True))
+    l_mine = l_in.at[y * 2 + c]
+    for w in range(TERMS):
+        switch = lanes_of(active[0][w : w + 1], active[1][w : w + 1]).astype(jnp.bfloat16)
+        rows = (packed_term(lband, w, masks) * switch).T
+        l_in[y * 2 + c, w] = jnp.concatenate([rows[:TILE], rows[TILE:]], axis=1)
+    masks = pack_masks(rsec, bond * 2)
+    for w in range(TERMS):
+        r_out[w] = packed_term(rband, w, masks)
+    mine[...] = jnp.zeros_like(mine)
+    out[...] = jnp.zeros_like(out)
     pl.semaphore_wait(barrier, 31)
 
     above = as_int((z == 3) & (c == 1))
@@ -147,23 +163,10 @@
                 psi1_r.at[halo_y * 4 + halo_slot], device(x, dy, halo_z, k),
             ).start()
 
-    masks = pack_masks(lsec, bond * 2)
-    number = lax.broadcasted_iota(jnp.int32, terms.shape, 1)
-    active = []
-    for h in range(2):
-        same = 1 - jnp.clip(jnp.abs(number - lsec[bond * 2 + h]), 0, 1)
-        active.append(jnp.sum(terms[...] * same, axis=1, keepdims=True))
-    l_mine = l_in.at[y * 2 + c]
-    for w in range(TERMS):
-        switch = lanes_of(active[0][w : w + 1], active[1][w : w + 1]).astype(jnp.bfloat16)
-        rows = (packed_term(lband, w, masks) * switch).T
-        l_in[y * 2 + c, w] = jnp.concatenate([rows[:TILE], rows[TILE:]], axis=1)
-    for d in range(1, 4):
-        remote(l_mine, l_mine, l_s.at[d - 1], l_r.at[d], device(x, turn(y, d), z, c)).start()
-
-    masks = pack_masks(rsec, bond * 2)
-    for w in range(TERMS):
-        r_out[w] = packed_term(rband, w, masks)
+    remote(l_mine, l_mine, l_s.at[0], l_r.at[1], device(x, turn(y, 1), z, c)).start()
+    remote(l_mine, l_mine, l_s.at[1], l_r.at[3], device(x, turn(y, -1), z, c)).start()
+    remote(l_mine, l_mine, lt_s.at[0], lt_r.at[0], twin).start()
+
     r_slot = lax.rem(z, 2) * 2 + c
 
     @pl.when(c == z // 2)
@@ -174,9 +177,9 @@
     def _():
         remote(r_out, r_in.at[r_slot], r_s.at[0], r_r.at[r_slot], twin).start()
 
-    for d in range(1, 4):
+    for n, d in enumerate((1, -1)):
         remote(
-            r_out, r_in.at[r_slot], r_s.at[d], r_r.at[r_slot], device(x, y, turn(z, d), z // 2)
+            r_out, r_in.at[r_slot], r_s.at[1 + n], r_r.at[r_slot], device(x, y, turn(z, d), z // 2)
         ).start()
 
     order = [0, 1, 3, 2]
@@ -185,14 +188,54 @@
         for slot in range(4):
             arrived(psi_in.at[group, slot, x], psi1_r.at[group * 4 + slot])
         part = psi_in.at[group, :, x]
-        for d in range(1, 4):
+        for n, d in enumerate((1, -1)):
             remote(
-                part, part, psi2_s.at[3 * k + d - 1], psi2_r.at[4 * (d - 1) + group],
+                part, part, psi2_s.at[2 * k + n], psi2_r.at[4 * n + group],
                 device(turn(x, d), y, z, c),
             ).start()
 
-    mine[...] = jnp.zeros_like(mine)
-    out[...] = jnp.zeros_like(out)
+    def psi_further(k):
+        d = k + k // 2 - 2 * (k // 3)
+        group = turn(y, -d)
+        for n, d in enumerate((1, -1)):
+            arrived(psi_in.at[group, :, turn(x, -d)], psi2_r.at[4 * n + group])
+            part = psi_in.at[group, 2 * n : 2 * n + 2, turn(x, -d)]
+            remote(
+                part, part, psi2_s.at[8 + 2 * k + n], psi2_r.at[8 + 4 * n + group],
+                device(turn(x, d), y, z, c),
+            ).start()
+
+    def left_further():
+        for n, d in enumerate((1, -1)):
+            came = turn(y, -d) * 2 + c
+            arrived(l_in.at[came], l_r.at[2 - d])
+            remote(l_in.at[came], l_in.at[came], lt_s.at[2 - d], lt_r.at[2 - d], twin).start()
+            part = l_in.at[came, :, 32 * n : 32 * n + 32]
+            remote(
+                part, part, l_s.at[2 + n], l_r.at[4 + n], device(x, turn(y, d), z, c)
+            ).start()
+
+    near = turn(z, (1 - 2 * lax.rem(z, 2)) * (1 - 2 * as_int(c != z // 2)))
+    onward = turn(z, z - near)
+    near_pair = lax.rem(near, 2) * 2
+    half = as_int(onward != turn(z, 1))
+
+    def right_part(first, which):
+        return r_in.at[
+            pl.ds(first, 2), :, pl.ds(pl.multiple_of(which * 96, 32), 96)
+        ]
+
+    def right_further():
+        for n in range(2):
+            arrived(r_in.at[near_pair + n], r_r.at[near_pair + n])
+        part = right_part(near_pair, half)
+        remote(part, part, r_s.at[3], rf_r.at[half], device(x, y, onward, c)).start()
+
+    psi_further(0)
+    psi_further(1)
+    left_further()
+    right_further()
+
     gram_at = {}
     row = 5
     for k in range(4):
@@ -256,13 +299,20 @@
         group = turn(y, -d)
         own = l_in.at[group * 2 + c]
 
-        @pl.when(k > 0)
+        @pl.when(k < 2)
         def _():
-            arrived(own, l_r.at[d])
-
-        remote(own, own, lt_s.at[d], lt_r.at[d], twin).start()
-        for e in range(1, 4):
-            arrived(psi_in.at[group, :, turn(x, -e)], psi2_r.at[4 * (e - 1) + group])
+            psi_further(k + 2)
+
+        @pl.when(k == 3)
+        def _():
+            for n in range(2):
+                arrived(l_in.at[group * 2 + c, :, 32 * n : 32 * n + 32], l_r.at[4 + n])
+            remote(own, own, lt_s.at[d], lt_r.at[d], twin).start()
+
+        for n in range(2):
+            arrived(
+                psi_in.at[group, 2 * n : 2 * n + 2, turn(x, 2)], psi2_r.at[8 + 4 * n + group]
+            )
         arrived(l_in.at[group * 2 + 1 - c], lt_r.at[d])
         left_shard(group, 0)
         left_shard(group, 1)
@@ -270,8 +320,34 @@
 
     lax.fori_loop(0, 4, left_step, 0)
 
+    for d in range(4):
+        zt = turn(z, d)
+        part = sub.at[:, pl.ds(pl.multiple_of(zt * 256, 256), 256)]
+        if d == 0:
+            @pl.when(c == z // 2)
+            def _(part=part):
+                pltpu.make_async_copy(part, sub_in.at[r_slot], sub_r.at[r_slot]).start()
+
+            @pl.when(c != z // 2)
+            def _(part=part):
+                remote(part, sub_in.at[r_slot], sub_s.at[0], sub_r.at[r_slot], twin).start()
+        else:
+            remote(
+                part, sub_in.at[r_slot], sub_s.at[d], sub_r.at[r_slot], device(x, y, zt, z // 2)
+            ).start()
+
+    @pl.when(c == z // 2)
+    def _():
+        first = lax.rem(z, 2) * 2
+        for n in range(2):
+            arrived(r_in.at[first + n], r_r.at[first + n])
+
+    @pl.when(c != z // 2)
+    def _():
+        for n in range(2):
+            arrived(right_part(lax.rem(z, 2) * 2, n), rf_r.at[n])
+
     for b in range(4):
-        arrived(r_in.at[b], r_r.at[b])
         place = [place_in_sector(rsec, y * 16 + c * 8 + b * 2 + h) for h in range(2)]
         weights = {}
         for i in range(6):
@@ -306,11 +382,13 @@
         rows = pl.ds(pl.multiple_of(g * 256, 256), 256)
         right_block(g, 0)
         right_block(g, 3)
+        halo_out[0, rows] = out[rows, 0:128].astype(jnp.bfloat16)
+        halo_out[1, rows] = out[rows, 640:768].astype(jnp.bfloat16)
         remote(
-            out.at[rows, 0:128], halo_in.at[1, rows], halo_s.at[i], halo_r.at[4 + i], left_next
+            halo_out.at[0, rows], halo_in.at[1, rows], halo_s.at[i], halo_r.at[4 + i], left_next
         ).start()
         remote(
-            out.at[rows, 640:768], halo_in.at[0, rows], halo_s.at[4 + i], halo_r.at[i], right_next
+            halo_out.at[1, rows], halo_in.at[0, rows], halo_s.at[4 + i], halo_r.at[i], right_next
         ).start()
         return carry
 
@@ -323,10 +401,10 @@
         for side in range(2):
             arrived(halo_in.at[side, rows], halo_r.at[4 * side + i])
         return [
-            out[rows, 128:256] + halo_in[0, rows],
+            out[rows, 128:256] + halo_in[0, rows].astype(jnp.float32),
             out[rows, 256:384],
             out[rows, 384:512],
-            out[rows, 512:640] + halo_in[1, rows],
+            out[rows, 512:640] + halo_in[1, rows].astype(jnp.float32),
         ]
 
     def inner_step(i, carry):
@@ -341,11 +419,18 @@
     for i in range(3):
         arrived(rs_in.at[i], rs_r.at[i])
     place_rows = pl.ds(pl.multiple_of(z * 256, 256), 256)
+    held = [jnp.zeros((8, 128), jnp.float32) for _ in range(5)]
     for b in range(4):
         lanes = slice(b * 128, (b + 1) * 128)
         total = kept[b]
         for i in range(3):
             total = total + rs_in[i, :, lanes].astype(jnp.float32)
+        arrived(sub_in.at[b], sub_r.at[b])
+        products = [total * total] + [
+            sub_in[b, k].astype(jnp.float32) * total for k in range(4)
+        ]
+        for k in range(5):
+            held[k] = held[k] + jnp.sum(products[k].reshape(32, 8, 128), axis=0)
         zt, ct = 2 * c + b // 2, b % 2
         here = (z == zt) & (c == ct)
 
@@ -360,21 +445,6 @@
                 deal.at[b], app.at[place_rows], deal_s.at[b], deal_r.at[z], device(x, y, zt, ct)
             ).start()
 
-    def sums(i, held):
-        rows = pl.ds(pl.multiple_of(i * 256, 256), 256)
-
-        @pl.when(jnp.logical_not((z == i) & (c == z // 2)))
-        def _():
-            arrived(app.at[rows], deal_r.at[i])
-
-        block = app[rows]
-        new = [held[0] + jnp.sum((block * block).reshape(32, 8, 128), axis=0)]
-        for k in range(4):
-            product = sub[k, rows, :].astype(jnp.float32) * block
-            new.append(held[k + 1] + jnp.sum(product.reshape(32, 8, 128), axis=0))
-        return tuple(new)
-
-    held = lax.fori_loop(0, 4, sums, tuple(jnp.zeros((8, 128), jnp.float32) for _ in range(5)))
     for k in range(5):
         mine[k : k + 1, :] = jnp.sum(held[k], axis=0, keepdims=True)
 
@@ -429,6 +499,11 @@
         vector_ref[rows, :] = residual * scale
         return carry
 
+    for i in range(4):
+        @pl.when(jnp.logical_not((z == i) & (c == z // 2)))
+        def _(i=i):
+            arrived(app.at[i * 256 : (i + 1) * 256], deal_r.at[i])
+
     lax.fori_loop(0, 8, write, 0)
 
     for n in range(8):
@@ -443,17 +518,23 @@
     @pl.when(c != z // 2)
     def _():
         left(r_out, r_s.at[0])
+        left(sub.at[:, 0:256], sub_s.at[0])
 
     for d in range(1, 4):
-        left(r_out, r_s.at[d])
-        left(l_mine, l_s.at[d - 1])
+        left(sub.at[:, 0:256], sub_s.at[d])
         left(rs_out.at[d - 1], rs_s.at[d - 1])
-    for n in range(12):
+    for n in range(8):
         left(psi_in.at[0, :, x], psi2_s.at[n])
+        left(psi_in.at[0, 0:2, x], psi2_s.at[8 + n])
+    for n in range(2):
+        left(l_mine, l_s.at[n])
+        left(l_in.at[0, :, 0:32], l_s.at[2 + n])
+        left(r_out, r_s.at[1 + n])
+    left(right_part(near_pair, half), r_s.at[3])
     for g in range(4):
         left(l_mine, lt_s.at[g])
-        left(out.at[0:256, 0:128], halo_s.at[g])
-        left(out.at[0:256, 640:768], halo_s.at[4 + g])
+        left(halo_out.at[0, 0:256], halo_s.at[g])
+        left(halo_out.at[1, 0:256], halo_s.at[4 + g])
         zt, ct = 2 * c + g // 2, g % 2
 
         @pl.when(jnp.logical_not((z == zt) & (c == ct)))
@@ -482,18 +563,20 @@
             pltpu.VMEM((4, 384, TERMS * 128), bf16),
             pltpu.VMEM((TERMS, 1024, 512), bf16),
             pltpu.VMEM((1024, 768), f32),
-            pltpu.VMEM((2, 1024, 128), f32),
+            pltpu.VMEM((2, 1024, 128), bf16),
+            pltpu.VMEM((2, 1024, 128), bf16),
             pltpu.VMEM((3, 256, 512), bf16),
             pltpu.VMEM((3, 256, 512), bf16),
+            pltpu.VMEM((4, 4, 256, 128), bf16),
             pltpu.VMEM((4, 256, 128), f32),
             pltpu.VMEM((1024, 128), f32),
             pltpu.VMEM((16, 128), f32),
             pltpu.VMEM((7, 16, 128), f32),
             pltpu.VMEM((16, 128), f32),
             pltpu.VMEM((15, 16, 128), f32),
-            dma((16,)), dma((16,)), dma((12,)), dma((12,)),
-            dma((4,)), dma((4,)), dma((3,)), dma((4,)), dma((4,)), dma((4,)),
-            dma((8,)), dma((8,)), dma((3,)), dma((3,)), dma((4,)), dma((4,)),
+            dma((16,)), dma((16,)), dma((16,)), dma((16,)),
+            dma((4,)), dma((4,)), dma((2,)), dma((4,)), dma((6,)), dma((4,)), dma((4,)),
+            dma((8,)), dma((8,)), dma((3,)), dma((3,)), dma((4,)), dma((4,)), dma((4,)), dma((4,)),
             dma((7,)), dma((7,)), dma((15,)), dma((15,)),
         ],
         compiler_params=pltpu.CompilerParams(

time: 89.5 us -> 79 us (0.88)
  Pallas kernels: 85.9 us -> 75.5 us
    pallas_call x1, Pallas kernels: 85.9 us -> 75.5 us  [per_device(): pl.pallas_call(kernel, out_shape=(shape, shape), in_specs=[smem, smem, vm...]
where the time goes in v4:
time: 79 us; the launch traced here: 78.8 us
  Pallas kernels  75.5 us (96%)
  local copies, waits for them, and re-layouts  2.72 us (3%)
    pallas_call x1, Pallas kernels, per_device(): pl.pallas_call(kernel, out_shape=(shape, shape), in_specs=[smem, smem, vm...  75.5 us
    unnamed x4, local copies, waits for them, and re-layouts  2.72 us

profile of v4, /device:TPU:1, one launch (start us, length us, event | category | flops | bytes accessed | tf_op | source)
XLA Modules:
  0.0 78.8 jit_solution(4464415275845958165)
XLA Ops:
  0.6 75.5 %two_site_step.1 = (f32[1024,128]{1,0:T(8,128)}, f32[1024,128]{1,0:T(8,128)}) custom-call(s32[64]{0:T(128)} %lsec.1, s32[64]{0:T(128)} %rsec.1, s32[9,32]{1,0:T(8,128)} %terms.1, bf16[128,4096]{1,0:T(8,128)(2,1)} %psi.1, bf16[4,1024,128]{2,1,0:T(8,128)(2,1)} %sub.1, bf16[9,320,128]{2,1,0:T(8,128)(2,1)} %bitcast.2, bf16[9,320,128]{2,1,0:T(8,128)(2,1)} %bitcast.3), custom_call_target="tpu_custom_call" | custom-call | tf_op jit(solution)/shard_map/two_site_step/pallas_call | solution.py:553
  76.1 0.0 copy-start
  76.1 1.9 %copy.11 = f32[1024,128]{1,0:T(8,128)} copy(f32[1024,128]{1,0:T(8,128)} %get-tuple-element.4) | data formatting | bytes 1048576
  78.0 0.0 copy-done
  78.0 0.8 %copy.12 = f32[1024,128]{1,0:T(8,128)} copy(f32[1024,128]{1,0:T(8,128)S(1)} %copy-done) | data formatting | bytes 1048576
Async XLA Ops:
  76.1 1.9 %copy-start = (f32[1024,128]{1,0:T(8,128)S(1)}, f32[1024,128]{1,0:T(8,128)}, u32[]{:S(2)}) copy-start(f32[1024,128]{1,0:T(8,128)} %get-tuple-element.5) | copy-start | bytes 1572868

commit v5 on v4

--- a/solution.py
+++ b/solution.py
@@ -377,7 +377,7 @@
     left_next = device(x, turn(y, -1 * as_int(c == 0)), z, 1 - c)
     right_next = device(x, turn(y, as_int(c == 1)), z, 1 - c)
 
-    def outer_step(i, carry):
+    def right_step(i, carry):
         g = turn(x, i + 1)
         rows = pl.ds(pl.multiple_of(g * 256, 256), 256)
         right_block(g, 0)
@@ -390,90 +390,105 @@
         remote(
             halo_out.at[1, rows], halo_in.at[0, rows], halo_s.at[4 + i], halo_r.at[i], right_next
         ).start()
-        return carry
-
-    lax.fori_loop(0, 4, outer_step, 0)
-
-    def columns_done(i, g):
-        rows = pl.ds(pl.multiple_of(g * 256, 256), 256)
         right_block(g, 1)
         right_block(g, 2)
+
+        @pl.when(i < 3)
+        def _():
+            rs_out[0, i] = out[rows, 256:512].astype(jnp.bfloat16)
+            remote(
+                rs_out.at[0, i], rs_in.at[0, i], rs_s.at[i], rs_r.at[i], device(g, y, z, c)
+            ).start()
+
+        return carry
+
+    lax.fori_loop(0, 4, right_step, 0)
+
+    def edge_columns(i, g):
+        rows = pl.ds(pl.multiple_of(g * 256, 256), 256)
         for side in range(2):
             arrived(halo_in.at[side, rows], halo_r.at[4 * side + i])
-        return [
+        return (
             out[rows, 128:256] + halo_in[0, rows].astype(jnp.float32),
-            out[rows, 256:384],
-            out[rows, 384:512],
             out[rows, 512:640] + halo_in[1, rows].astype(jnp.float32),
-        ]
-
-    def inner_step(i, carry):
+        )
+
+    def edge_step(i, carry):
         g = turn(x, i + 1)
-        for b, total in enumerate(columns_done(i, g)):
-            rs_out[i, :, b * 128 : (b + 1) * 128] = total.astype(jnp.bfloat16)
-        remote(rs_out.at[i], rs_in.at[i], rs_s.at[i], rs_r.at[i], device(g, y, z, c)).start()
+        for n, total in enumerate(edge_columns(i, g)):
+            rs_out[1, i, :, n * 128 : (n + 1) * 128] = total.astype(jnp.bfloat16)
+        remote(
+            rs_out.at[1, i], rs_in.at[1, i], rs_s.at[3 + i], rs_r.at[3 + i], device(g, y, z, c)
+        ).start()
         return carry
 
-    lax.fori_loop(0, 3, inner_step, 0)
-    kept = columns_done(3, x)
-    for i in range(3):
-        arrived(rs_in.at[i], rs_r.at[i])
+    lax.fori_loop(0, 3, edge_step, 0)
+
+    own_group = pl.ds(pl.multiple_of(x * 256, 256), 256)
     place_rows = pl.ds(pl.multiple_of(z * 256, 256), 256)
     held = [jnp.zeros((8, 128), jnp.float32) for _ in range(5)]
-    for b in range(4):
-        lanes = slice(b * 128, (b + 1) * 128)
-        total = kept[b]
+    for turn_of in range(2):
+        if turn_of == 0:
+            kept = (out[own_group, 256:384], out[own_group, 384:512])
+        else:
+            kept = edge_columns(3, x)
         for i in range(3):
-            total = total + rs_in[i, :, lanes].astype(jnp.float32)
-        arrived(sub_in.at[b], sub_r.at[b])
-        products = [total * total] + [
-            sub_in[b, k].astype(jnp.float32) * total for k in range(4)
-        ]
-        for k in range(5):
-            held[k] = held[k] + jnp.sum(products[k].reshape(32, 8, 128), axis=0)
-        zt, ct = 2 * c + b // 2, b % 2
-        here = (z == zt) & (c == ct)
-
-        @pl.when(here)
-        def _(total=total):
-            app[place_rows] = total
-
-        @pl.when(jnp.logical_not(here))
-        def _(total=total, b=b, zt=zt, ct=ct):
-            deal[b] = total
-            remote(
-                deal.at[b], app.at[place_rows], deal_s.at[b], deal_r.at[z], device(x, y, zt, ct)
-            ).start()
-
+            arrived(rs_in.at[turn_of, i], rs_r.at[3 * turn_of + i])
+        for n in range(2):
+            b = (1 + n) if turn_of == 0 else 3 * n
+            total = kept[n]
+            for i in range(3):
+                total = total + rs_in[turn_of, i, :, n * 128 : (n + 1) * 128].astype(jnp.float32)
+            zt, ct = 2 * c + b // 2, b % 2
+            here = (z == zt) & (c == ct)
+
+            @pl.when(here)
+            def _(total=total):
+                app[place_rows] = total
+
+            @pl.when(jnp.logical_not(here))
+            def _(total=total, b=b, zt=zt, ct=ct):
+                deal[b] = total
+                remote(
+                    deal.at[b], app.at[place_rows], deal_s.at[b], deal_r.at[z],
+                    device(x, y, zt, ct),
+                ).start()
+
+            arrived(sub_in.at[b], sub_r.at[b])
+            products = [total * total] + [
+                sub_in[b, k].astype(jnp.float32) * total for k in range(4)
+            ]
+            for k in range(5):
+                held[k] = held[k] + jnp.sum(products[k].reshape(32, 8, 128), axis=0)
     for k in range(5):
         mine[k : k + 1, :] = jnp.sum(held[k], axis=0, keepdims=True)
 
+    copies = []
+    for d in range(1, 16):
+        other = lax.rem(x * 4 + y + d, 16)
+        copy = remote(
+            mine, first_in.at[d - 1], send_c.at[d - 1], recv_c.at[d - 1],
+            (other // 4, lax.rem(other, 4) * 8 + q),
+        )
+        copy.start()
+        copies.append(copy)
+    for copy in copies:
+        copy.wait()
+    added = mine[...]
+    for d in range(15):
+        added = added + first_in[d]
+    second_out[...] = added
     copies = []
     for d in range(1, 8):
         copy = remote(
-            mine, first_in.at[d - 1], send_c.at[d - 1], recv_c.at[d - 1],
+            second_out, second_in.at[d - 1], send_d.at[d - 1], recv_d.at[d - 1],
             (x, y * 8 + lax.rem(q + d, 8)),
         )
         copy.start()
         copies.append(copy)
     for copy in copies:
         copy.wait()
-    added = mine[...]
     for d in range(7):
-        added = added + first_in[d]
-    second_out[...] = added
-    copies = []
-    for d in range(1, 16):
-        other = lax.rem(x * 4 + y + d, 16)
-        copy = remote(
-            second_out, second_in.at[d - 1], send_d.at[d - 1], recv_d.at[d - 1],
-            (other // 4, lax.rem(other, 4) * 8 + q),
-        )
-        copy.start()
-        copies.append(copy)
-    for copy in copies:
-        copy.wait()
-    for d in range(15):
         added = added + second_in[d]
     sums_all = jnp.sum(added, axis=1, keepdims=True)
 
@@ -522,7 +537,8 @@
 
     for d in range(1, 4):
         left(sub.at[:, 0:256], sub_s.at[d])
-        left(rs_out.at[d - 1], rs_s.at[d - 1])
+        left(rs_out.at[0, d - 1], rs_s.at[d - 1])
+        left(rs_out.at[1, d - 1], rs_s.at[2 + d])
     for n in range(8):
         left(psi_in.at[0, :, x], psi2_s.at[n])
         left(psi_in.at[0, 0:2, x], psi2_s.at[8 + n])
@@ -565,19 +581,19 @@
             pltpu.VMEM((1024, 768), f32),
             pltpu.VMEM((2, 1024, 128), bf16),
             pltpu.VMEM((2, 1024, 128), bf16),
-            pltpu.VMEM((3, 256, 512), bf16),
-            pltpu.VMEM((3, 256, 512), bf16),
+            pltpu.VMEM((2, 3, 256, 256), bf16),
+            pltpu.VMEM((2, 3, 256, 256), bf16),
             pltpu.VMEM((4, 4, 256, 128), bf16),
             pltpu.VMEM((4, 256, 128), f32),
             pltpu.VMEM((1024, 128), f32),
             pltpu.VMEM((16, 128), f32),
+            pltpu.VMEM((15, 16, 128), f32),
+            pltpu.VMEM((16, 128), f32),
             pltpu.VMEM((7, 16, 128), f32),
-            pltpu.VMEM((16, 128), f32),
-            pltpu.VMEM((15, 16, 128), f32),
             dma((16,)), dma((16,)), dma((16,)), dma((16,)),
             dma((4,)), dma((4,)), dma((2,)), dma((4,)), dma((6,)), dma((4,)), dma((4,)),
-            dma((8,)), dma((8,)), dma((3,)), dma((3,)), dma((4,)), dma((4,)), dma((4,)), dma((4,)),
-            dma((7,)), dma((7,)), dma((15,)), dma((15,)),
+            dma((8,)), dma((8,)), dma((6,)), dma((6,)), dma((4,)), dma((4,)), dma((4,)), dma((4,)),
+            dma((15,)), dma((15,)), dma((7,)), dma((7,)),
         ],
         compiler_params=pltpu.CompilerParams(
             collective_id=0, has_side_effects=True, vmem_limit_bytes=56 * 1024 * 1024

time: 79 us -> 73.8 us (0.934)
  Pallas kernels: 75.5 us -> 70.3 us
    pallas_call x1, Pallas kernels: 75.5 us -> 70.3 us  [per_device(): pl.pallas_call(kernel, out_shape=(shape, shape), in_specs=[smem, smem, vm...]
where the time goes in v5:
time: 73.8 us; the launch traced here: 73.7 us
  Pallas kernels  70.3 us (95%)
  local copies, waits for them, and re-layouts  2.72 us (4%)
    pallas_call x1, Pallas kernels, per_device(): pl.pallas_call(kernel, out_shape=(shape, shape), in_specs=[smem, smem, vm...  70.3 us
    unnamed x4, local copies, waits for them, and re-layouts  2.72 us

profile of v5, /device:TPU:1, one launch (start us, length us, event | category | flops | bytes accessed | tf_op | source)
XLA Modules:
  0.0 73.7 jit_solution(18396286395909547413)
XLA Ops:
  0.6 70.3 %two_site_step.1 = (f32[1024,128]{1,0:T(8,128)}, f32[1024,128]{1,0:T(8,128)}) custom-call(s32[64]{0:T(128)} %lsec.1, s32[64]{0:T(128)} %rsec.1, s32[9,32]{1,0:T(8,128)} %terms.1, bf16[128,4096]{1,0:T(8,128)(2,1)} %psi.1, bf16[4,1024,128]{2,1,0:T(8,128)(2,1)} %sub.1, bf16[9,320,128]{2,1,0:T(8,128)(2,1)} %bitcast.2, bf16[9,320,128]{2,1,0:T(8,128)(2,1)} %bitcast.3), custom_call_target="tpu_custom_call" | custom-call | tf_op jit(solution)/shard_map/two_site_step/pallas_call | solution.py:569
  70.9 0.0 copy-start
  70.9 1.9 %copy.11 = f32[1024,128]{1,0:T(8,128)} copy(f32[1024,128]{1,0:T(8,128)} %get-tuple-element.4) | data formatting | bytes 1048576
  72.9 0.0 copy-done
  72.9 0.8 %copy.12 = f32[1024,128]{1,0:T(8,128)} copy(f32[1024,128]{1,0:T(8,128)S(1)} %copy-done) | data formatting | bytes 1048576
Async XLA Ops:
  70.9 1.9 %copy-start = (f32[1024,128]{1,0:T(8,128)S(1)}, f32[1024,128]{1,0:T(8,128)}, u32[]{:S(2)}) copy-start(f32[1024,128]{1,0:T(8,128)} %get-tuple-element.5) | copy-start | bytes 1572868

commit v6 on v5

--- a/solution.py
+++ b/solution.py
@@ -65,7 +65,7 @@
     lsec, rsec, terms, psi, sub, lband, rband,
     applied_ref, vector_ref,
     l_in, r_out, r_in, psi_in, r_wide, mid, out, halo_out, halo_in, rs_out, rs_in, sub_in, deal, app,
-    mine, first_in, second_out, second_in,
+    mine, folded, first_in, second_out, second_in,
     psi1_s, psi1_r, psi2_s, psi2_r, r_s, r_r, rf_r, l_s, l_r, lt_s, lt_r,
     halo_s, halo_r, rs_s, rs_r, sub_s, sub_r, deal_s, deal_r, send_c, recv_c, send_d, recv_d,
 ):
@@ -134,33 +134,47 @@
     halo_slot = 3 * (1 - c)
     own_rows = pl.ds(pl.multiple_of(x * 32, 32), 32)
 
+    def psi_columns(dy, k):
+        return pl.ds(pl.multiple_of(dy * 1024 + k * 512, 512), 512)
+
     def psi_part(dy, k):
-        return psi.at[own_rows, pl.ds(pl.multiple_of(dy * 1024 + k * 512, 512), 512)]
-
-    for d in range(4):
+        return psi.at[own_rows, psi_columns(dy, k)]
+
+    def psi_whole(dy, k):
+        return psi.at[:, psi_columns(dy, k)]
+
+    def psi_quarter(group, slot, part):
+        return psi_in.at[group, slot, pl.ds(pl.multiple_of(part * 32, 32), 32)]
+
+    for k in range(2):
+        @pl.when(c == k)
+        def _(k=k):
+            pltpu.make_async_copy(
+                psi_whole(y, k), psi_in.at[y, 1 + c], psi1_r.at[y * 4 + 1 + c]
+            ).start()
+
+        @pl.when(c != k)
+        def _(k=k):
+            remote(
+                psi_whole(y, k), psi_in.at[y, 1 + c], psi1_s.at[k], psi1_r.at[y * 4 + 1 + c], twin
+            ).start()
+
+    for d in (1, 3, 2, 0):
         dy = turn(y, d)
+        hy = turn(halo_y, d)
         for k in range(2):
             n = 2 * d + k
-            own = psi_in.at[y, 1 + c, x]
-            if d == 0:
-                @pl.when(c == k)
-                def _(k=k, own=own, dy=dy):
-                    pltpu.make_async_copy(psi_part(dy, k), own, psi1_r.at[y * 4 + 1 + c]).start()
-
-                @pl.when(c != k)
-                def _(k=k, own=own, dy=dy, n=n):
-                    remote(
-                        psi_part(dy, k), own, psi1_s.at[n], psi1_r.at[y * 4 + 1 + c],
-                        device(x, dy, z, k),
-                    ).start()
+            if d > 0:
+                remote(
+                    psi_part(dy, k), psi_quarter(y, 1 + c, x), psi1_s.at[n],
+                    psi1_r.at[y * 4 + 1 + c], device(x, dy, z, k),
+                ).start()
+                source, target = psi_part(hy, k), psi_quarter(halo_y, halo_slot, x)
             else:
-                remote(
-                    psi_part(dy, k), own, psi1_s.at[n], psi1_r.at[y * 4 + 1 + c],
-                    device(x, dy, z, k),
-                ).start()
+                source, target = psi_whole(hy, k), psi_in.at[halo_y, halo_slot]
             remote(
-                psi_part(dy, k), psi_in.at[halo_y, halo_slot, x], psi1_s.at[8 + n],
-                psi1_r.at[halo_y * 4 + halo_slot], device(x, dy, halo_z, k),
+                source, target, psi1_s.at[8 + n], psi1_r.at[halo_y * 4 + halo_slot],
+                device(x, hy, halo_z, k),
             ).start()
 
     remote(l_mine, l_mine, l_s.at[0], l_r.at[1], device(x, turn(y, 1), z, c)).start()
@@ -183,11 +197,15 @@
         ).start()
 
     order = [0, 1, 3, 2]
-    for k in range(4):
+
+    def psi_strip(group, first, last, part):
+        return psi_in.at[group, first:last, pl.ds(pl.multiple_of(part * 32, 32), 32)]
+
+    def psi_second(k):
         group = turn(y, -order[k])
         for slot in range(4):
-            arrived(psi_in.at[group, slot, x], psi1_r.at[group * 4 + slot])
-        part = psi_in.at[group, :, x]
+            arrived(psi_quarter(group, slot, x), psi1_r.at[group * 4 + slot])
+        part = psi_strip(group, 0, 4, x)
         for n, d in enumerate((1, -1)):
             remote(
                 part, part, psi2_s.at[2 * k + n], psi2_r.at[4 * n + group],
@@ -198,8 +216,8 @@
         d = k + k // 2 - 2 * (k // 3)
         group = turn(y, -d)
         for n, d in enumerate((1, -1)):
-            arrived(psi_in.at[group, :, turn(x, -d)], psi2_r.at[4 * n + group])
-            part = psi_in.at[group, 2 * n : 2 * n + 2, turn(x, -d)]
+            arrived(psi_strip(group, 0, 4, turn(x, -d)), psi2_r.at[4 * n + group])
+            part = psi_strip(group, 2 * n, 2 * n + 2, turn(x, -d))
             remote(
                 part, part, psi2_s.at[8 + 2 * k + n], psi2_r.at[8 + 4 * n + group],
                 device(turn(x, d), y, z, c),
@@ -231,8 +249,10 @@
         part = right_part(near_pair, half)
         remote(part, part, r_s.at[3], rf_r.at[half], device(x, y, onward, c)).start()
 
-    psi_further(0)
+    psi_second(1)
+    psi_second(2)
     psi_further(1)
+    psi_second(3)
     left_further()
     right_further()
 
@@ -274,9 +294,7 @@
             for n in range(2):
                 lanes = slice(n * 256, (n + 1) * 256)
                 tiles = {
-                    t: jnp.concatenate(
-                        [psi_in[group, t // 2, (t % 2) * 2 + i, :, lanes] for i in range(2)], axis=0
-                    )
+                    t: psi_in[group, t // 2, (t % 2) * TILE : (t % 2 + 1) * TILE, lanes]
                     for t in range(first - 2, first + 3)
                 }
                 source = jnp.concatenate(
@@ -309,10 +327,18 @@
                 arrived(l_in.at[group * 2 + c, :, 32 * n : 32 * n + 32], l_r.at[4 + n])
             remote(own, own, lt_s.at[d], lt_r.at[d], twin).start()
 
-        for n in range(2):
-            arrived(
-                psi_in.at[group, 2 * n : 2 * n + 2, turn(x, 2)], psi2_r.at[8 + 4 * n + group]
-            )
+        @pl.when(k == 0)
+        def _():
+            for slot in range(4):
+                arrived(psi_in.at[y, slot], psi1_r.at[y * 4 + slot])
+
+        @pl.when(k > 0)
+        def _():
+            for n in range(2):
+                arrived(
+                    psi_strip(group, 2 * n, 2 * n + 2, turn(x, 2)), psi2_r.at[8 + 4 * n + group]
+                )
+
         arrived(l_in.at[group * 2 + 1 - c], lt_r.at[d])
         left_shard(group, 0)
         left_shard(group, 1)
@@ -462,19 +488,23 @@
                 held[k] = held[k] + jnp.sum(products[k].reshape(32, 8, 128), axis=0)
     for k in range(5):
         mine[k : k + 1, :] = jnp.sum(held[k], axis=0, keepdims=True)
+    both = mine[...]
+    both = both + pltpu.roll(both, TILE, 1)
+    low_lanes = lax.broadcasted_iota(jnp.int32, (8, 128), 1) < TILE
+    folded[...] = jnp.where(low_lanes, both[:8], both[8:])
 
     copies = []
     for d in range(1, 16):
         other = lax.rem(x * 4 + y + d, 16)
         copy = remote(
-            mine, first_in.at[d - 1], send_c.at[d - 1], recv_c.at[d - 1],
+            folded, first_in.at[d - 1], send_c.at[d - 1], recv_c.at[d - 1],
             (other // 4, lax.rem(other, 4) * 8 + q),
         )
         copy.start()
         copies.append(copy)
     for copy in copies:
         copy.wait()
-    added = mine[...]
+    added = folded[...]
     for d in range(15):
         added = added + first_in[d]
     second_out[...] = added
@@ -490,7 +520,13 @@
         copy.wait()
     for d in range(7):
         added = added + second_in[d]
-    sums_all = jnp.sum(added, axis=1, keepdims=True)
+    sums_all = jnp.concatenate(
+        [
+            jnp.sum(jnp.where(low_lanes, added, 0.0), axis=1, keepdims=True),
+            jnp.sum(jnp.where(low_lanes, 0.0, added), axis=1, keepdims=True),
+        ],
+        axis=0,
+    )
 
     def one(i):
         return sums_all[i : i + 1, :] * (1.0 / float(D_LEFT * D_RIGHT))
@@ -521,13 +557,14 @@
 
     lax.fori_loop(0, 8, write, 0)
 
-    for n in range(8):
-        if n < 2:
-            @pl.when(c != n)
-            def _(n=n):
-                left(psi_part(y, n), psi1_s.at[n])
-        else:
-            left(psi_part(y, 0), psi1_s.at[n])
+    for n in range(2):
+        @pl.when(c != n)
+        def _(n=n):
+            left(psi_whole(y, n), psi1_s.at[n])
+
+        left(psi_whole(y, n), psi1_s.at[8 + n])
+    for n in range(2, 8):
+        left(psi_part(y, 0), psi1_s.at[n])
         left(psi_part(y, 0), psi1_s.at[8 + n])
 
     @pl.when(c != z // 2)
@@ -539,9 +576,9 @@
         left(sub.at[:, 0:256], sub_s.at[d])
         left(rs_out.at[0, d - 1], rs_s.at[d - 1])
         left(rs_out.at[1, d - 1], rs_s.at[2 + d])
-    for n in range(8):
-        left(psi_in.at[0, :, x], psi2_s.at[n])
-        left(psi_in.at[0, 0:2, x], psi2_s.at[8 + n])
+    for n in range(2, 8):
+        left(psi_strip(0, 0, 4, x), psi2_s.at[n])
+        left(psi_strip(0, 0, 2, x), psi2_s.at[8 + n])
     for n in range(2):
         left(l_mine, l_s.at[n])
         left(l_in.at[0, :, 0:32], l_s.at[2 + n])
@@ -569,13 +606,13 @@
     return pl.pallas_call(
         kernel,
         out_shape=(shape, shape),
-        in_specs=[smem, smem, vmem, vmem, vmem, vmem, vmem],
+        in_specs=[smem, smem, vmem, pl.BlockSpec(memory_space=pl.ANY), vmem, vmem, vmem],
         out_specs=(vmem, vmem),
         scratch_shapes=[
             pltpu.VMEM((8, TERMS, TILE, 2 * PACKED), bf16),
             pltpu.VMEM((TERMS, PACKED, 128), bf16),
             pltpu.VMEM((4, TERMS, PACKED, 128), bf16),
-            pltpu.VMEM((4, 4, 4, 32, 512), bf16),
+            pltpu.VMEM((4, 4, 128, 512), bf16),
             pltpu.VMEM((4, 384, TERMS * 128), bf16),
             pltpu.VMEM((TERMS, 1024, 512), bf16),
             pltpu.VMEM((1024, 768), f32),
@@ -587,9 +624,10 @@
             pltpu.VMEM((4, 256, 128), f32),
             pltpu.VMEM((1024, 128), f32),
             pltpu.VMEM((16, 128), f32),
-            pltpu.VMEM((15, 16, 128), f32),
-            pltpu.VMEM((16, 128), f32),
-            pltpu.VMEM((7, 16, 128), f32),
+            pltpu.VMEM((8, 128), f32),
+            pltpu.VMEM((15, 8, 128), f32),
+            pltpu.VMEM((8, 128), f32),
+            pltpu.VMEM((7, 8, 128), f32),
             dma((16,)), dma((16,)), dma((16,)), dma((16,)),
             dma((4,)), dma((4,)), dma((2,)), dma((4,)), dma((6,)), dma((4,)), dma((4,)),
             dma((8,)), dma((8,)), dma((6,)), dma((6,)), dma((4,)), dma((4,)), dma((4,)), dma((4,)),

time: 73.8 us -> 71.9 us (0.974)
  Pallas kernels: 70.3 us -> 68.4 us
    pallas_call x1, Pallas kernels: 70.3 us -> 68.4 us  [per_device(): pl.pallas_call(kernel, out_shape=(shape, shape), in_specs=[smem, smem, vm...]
where the time goes in v6:
time: 71.9 us; the launch traced here: 71.8 us
  Pallas kernels  68.4 us (95%)
  local copies, waits for them, and re-layouts  2.72 us (4%)
    pallas_call x1, Pallas kernels, per_device(): pl.pallas_call(kernel, out_shape=(shape, shape), in_specs=[smem, smem, vm...  68.4 us
    unnamed x4, local copies, waits for them, and re-layouts  2.72 us

profile of v6, /device:TPU:1, one launch (start us, length us, event | category | flops | bytes accessed | tf_op | source)
XLA Modules:
  0.0 71.8 jit_solution(13442729804252917734)
XLA Ops:
  0.6 68.4 %two_site_step.1 = (f32[1024,128]{1,0:T(8,128)}, f32[1024,128]{1,0:T(8,128)}) custom-call(s32[64]{0:T(128)} %lsec.1, s32[64]{0:T(128)} %rsec.1, s32[9,32]{1,0:T(8,128)} %terms.1, bf16[128,4096]{1,0:T(8,128)(2,1)} %psi.1, bf16[4,1024,128]{2,1,0:T(8,128)(2,1)} %sub.1, bf16[9,320,128]{2,1,0:T(8,128)(2,1)} %bitcast.2, bf16[9,320,128]{2,1,0:T(8,128)(2,1)} %bitcast.3), custom_call_target="tpu_custom_call" | custom-call | tf_op jit(solution)/shard_map/two_site_step/pallas_call | solution.py:606
  69.1 0.0 copy-start
  69.1 1.9 %copy.11 = f32[1024,128]{1,0:T(8,128)} copy(f32[1024,128]{1,0:T(8,128)} %get-tuple-element.4) | data formatting | bytes 1048576
  71.0 0.0 copy-done
  71.0 0.8 %copy.12 = f32[1024,128]{1,0:T(8,128)} copy(f32[1024,128]{1,0:T(8,128)S(1)} %copy-done) | data formatting | bytes 1048576
Async XLA Ops:
  69.1 1.9 %copy-start = (f32[1024,128]{1,0:T(8,128)S(1)}, f32[1024,128]{1,0:T(8,128)}, u32[]{:S(2)}) copy-start(f32[1024,128]{1,0:T(8,128)} %get-tuple-element.5) | copy-start | bytes 1572868

commit v7 on v6

--- a/solution.py
+++ b/solution.py
@@ -63,8 +63,8 @@
 
 def kernel(
     lsec, rsec, terms, psi, sub, lband, rband,
-    applied_ref, vector_ref,
-    l_in, r_out, r_in, psi_in, r_wide, mid, out, halo_out, halo_in, rs_out, rs_in, sub_in, deal, app,
+    app, stats_ref,
+    l_in, r_out, r_in, psi_in, r_wide, mid, out, halo_out, halo_in, rs_out, rs_in, sub_in, deal,
     mine, folded, first_in, second_out, second_in,
     psi1_s, psi1_r, psi2_s, psi2_r, r_s, r_r, rf_r, l_s, l_r, lt_s, lt_r,
     halo_s, halo_r, rs_s, rs_r, sub_s, sub_r, deal_s, deal_r, send_c, recv_c, send_d, recv_d,
@@ -251,10 +251,10 @@
 
     psi_second(1)
     psi_second(2)
+    psi_second(3)
     psi_further(1)
-    psi_second(3)
+    right_further()
     left_further()
-    right_further()
 
     gram_at = {}
     row = 5
@@ -540,22 +540,14 @@
             energy = energy + twice * coefficient[k] * coefficient[m] * one(gram_at[k, m])
     scale = lax.rsqrt(jnp.maximum(energy, 0.0) + epsilon)
 
-    def write(i, carry):
-        rows = pl.ds(pl.multiple_of(i * 128, 128), 128)
-        block = app[rows]
-        residual = block
-        for k in range(4):
-            residual = residual - coefficient[k] * sub[k, rows, :].astype(jnp.float32)
-        applied_ref[rows, :] = block
-        vector_ref[rows, :] = residual * scale
-        return carry
-
     for i in range(4):
         @pl.when(jnp.logical_not((z == i) & (c == z // 2)))
         def _(i=i):
             arrived(app.at[i * 256 : (i + 1) * 256], deal_r.at[i])
 
-    lax.fori_loop(0, 8, write, 0)
+    for n, value in enumerate(coefficient + [scale]):
+        stats_ref[n : n + 1, :] = jnp.zeros((1, 128), jnp.float32) + value
+    stats_ref[5:8, :] = jnp.zeros((3, 128), jnp.float32)
 
     for n in range(2):
         @pl.when(c != n)
@@ -595,6 +587,14 @@
             left(deal.at[g], deal_s.at[g])
 
 
+def write_kernel(stats_ref, app_ref, sub_ref, applied_ref, vector_ref):
+    residual = app_ref[...]
+    applied_ref[...] = residual
+    for k in range(4):
+        residual = residual - stats_ref[k : k + 1, :] * sub_ref[k].astype(jnp.float32)
+    vector_ref[...] = residual * stats_ref[4:5, :]
+
+
 def per_device(
     wavefunction, subspace, left_band, right_band, left_sector, right_sector, term_sectors
 ):
@@ -603,9 +603,9 @@
     bf16, f32 = jnp.bfloat16, jnp.float32
     vmem = pl.BlockSpec(memory_space=pltpu.VMEM)
     smem = pl.BlockSpec(memory_space=pltpu.SMEM)
-    return pl.pallas_call(
+    app, stats = pl.pallas_call(
         kernel,
-        out_shape=(shape, shape),
+        out_shape=(shape, jax.ShapeDtypeStruct((8, 128), f32)),
         in_specs=[smem, smem, vmem, pl.BlockSpec(memory_space=pl.ANY), vmem, vmem, vmem],
         out_specs=(vmem, vmem),
         scratch_shapes=[
@@ -622,7 +622,6 @@
             pltpu.VMEM((2, 3, 256, 256), bf16),
             pltpu.VMEM((4, 4, 256, 128), bf16),
             pltpu.VMEM((4, 256, 128), f32),
-            pltpu.VMEM((1024, 128), f32),
             pltpu.VMEM((16, 128), f32),
             pltpu.VMEM((8, 128), f32),
             pltpu.VMEM((15, 8, 128), f32),
@@ -641,6 +640,20 @@
         left_sector, right_sector, term_sectors, wavefunction, subspace,
         jnp.swapaxes(left_band, 1, 2), jnp.swapaxes(right_band, 1, 2),
     )
+    each = 512
+    block = pl.BlockSpec((each, 128), lambda i: (i, 0))
+    return pl.pallas_call(
+        write_kernel,
+        grid=(1024 // each,),
+        out_shape=(shape, shape),
+        in_specs=[
+            pl.BlockSpec((8, 128), lambda i: (0, 0)),
+            block,
+            pl.BlockSpec((4, each, 128), lambda i: (0, i, 0)),
+        ],
+        out_specs=(block, block),
+        name="write_results",
+    )(stats, app, subspace)
 
 
 def solution(mesh):

time: 71.9 us -> 70.6 us (0.982)
  local copies, waits for them, and re-layouts: 2.72 us -> 0 us
  Pallas kernels: 68.4 us -> 69.8 us
    unnamed x4 -> x0, local copies, waits for them, and re-layouts: 2.72 us -> none
    pallas_call x1 -> x2, Pallas kernels: 68.4 us -> 69.8 us  [the longest x1 67.6 us: per_device(): pl.pallas_call(kernel, out_shape=(shape, jax.ShapeDtypeStruct((8, 128), f...]
where the time goes in v7:
time: 70.6 us; the launch traced here: 70.4 us
  Pallas kernels  69.8 us (99%)
    pallas_call x1, Pallas kernels, per_device(): pl.pallas_call(kernel, out_shape=(shape, jax.ShapeDtypeStruct((8, 128), f...  67.6 us
    pallas_call x1, Pallas kernels, per_device(): pl.pallas_call(write_kernel, grid=(1024 // each,), out_shape=(shape, shap...  2.21 us

profile of v7, /device:TPU:1, one launch (start us, length us, event | category | flops | bytes accessed | tf_op | source)
XLA Modules:
  0.0 70.4 jit_solution(13031735081286647743)
XLA Ops:
  0.6 67.6 %two_site_step.1 = (f32[1024,128]{1,0:T(8,128)}, f32[8,128]{1,0:T(8,128)}) custom-call(s32[64]{0:T(128)} %lsec.1, s32[64]{0:T(128)} %rsec.1, s32[9,32]{1,0:T(8,128)} %terms.1, bf16[128,4096]{1,0:T(8,128)(2,1)} %psi.1, bf16[4,1024,128]{2,1,0:T(8,128)(2,1)} %sub_ref.1, bf16[9,320,128]{2,1,0:T(8,128)(2,1)} %bitcast.2, bf16[9,320,128]{2,1,0:T(8,128)(2,1)} %bitcast.3), custom_call_target="tpu_custom_call" | custom-call | tf_op jit(solution)/shard_map/two_site_step/pallas_call | solution.py:606
  68.2 2.2 %write_results.1 = (f32[1024,128]{1,0:T(8,128)}, f32[1024,128]{1,0:T(8,128)}) custom-call(f32[8,128]{1,0:T(8,128)} %get-tuple-element.4.stats_ref, f32[1024,128]{1,0:T(8,128)} %get-tuple-element.5.app_ref, bf16[4,1024,128]{2,1,0:T(8,128)(2,1)} %sub_ref.1), custom_call_target="tpu_custom_call" | custom-call | tf_op jit(solution)/shard_map/write_results/pallas_call | solution.py:645

commit v8 on v7

--- a/solution.py
+++ b/solution.py
@@ -100,8 +100,6 @@
         pl.semaphore_signal(barrier, inc=1, device_id=target, device_id_type=MESH)
 
     barrier = pltpu.get_barrier_semaphore()
-    for d in range(1, 8):
-        signal((x, y * 8 + lax.rem(q + d, 8)))
     for d in range(1, 16):
         other = lax.rem(x * 4 + y + d, 16)
         signal((other // 4, lax.rem(other, 4) * 8 + q))
@@ -109,22 +107,12 @@
         signal(device(x, turn(y, d), z, 1 - c))
         signal(device(x, turn(y, d), turn(z, -1), 1))
         signal(device(x, turn(y, d), turn(z, 1), 0))
-    masks = pack_masks(lsec, bond * 2)
-    number = lax.broadcasted_iota(jnp.int32, terms.shape, 1)
-    active = []
-    for h in range(2):
-        same = 1 - jnp.clip(jnp.abs(number - lsec[bond * 2 + h]), 0, 1)
-        active.append(jnp.sum(terms[...] * same, axis=1, keepdims=True))
-    l_mine = l_in.at[y * 2 + c]
-    for w in range(TERMS):
-        switch = lanes_of(active[0][w : w + 1], active[1][w : w + 1]).astype(jnp.bfloat16)
-        rows = (packed_term(lband, w, masks) * switch).T
-        l_in[y * 2 + c, w] = jnp.concatenate([rows[:TILE], rows[TILE:]], axis=1)
+    for d in range(1, 8):
+        signal((x, y * 8 + lax.rem(q + d, 8)))
     masks = pack_masks(rsec, bond * 2)
     for w in range(TERMS):
         r_out[w] = packed_term(rband, w, masks)
     mine[...] = jnp.zeros_like(mine)
-    out[...] = jnp.zeros_like(out)
     pl.semaphore_wait(barrier, 31)
 
     above = as_int((z == 3) & (c == 1))
@@ -177,6 +165,17 @@
                 device(x, hy, halo_z, k),
             ).start()
 
+    masks = pack_masks(lsec, bond * 2)
+    number = lax.broadcasted_iota(jnp.int32, terms.shape, 1)
+    active = []
+    for h in range(2):
+        same = 1 - jnp.clip(jnp.abs(number - lsec[bond * 2 + h]), 0, 1)
+        active.append(jnp.sum(terms[...] * same, axis=1, keepdims=True))
+    l_mine = l_in.at[y * 2 + c]
+    for w in range(TERMS):
+        switch = lanes_of(active[0][w : w + 1], active[1][w : w + 1]).astype(jnp.bfloat16)
+        rows = (packed_term(lband, w, masks) * switch).T
+        l_in[y * 2 + c, w] = jnp.concatenate([rows[:TILE], rows[TILE:]], axis=1)
     remote(l_mine, l_mine, l_s.at[0], l_r.at[1], device(x, turn(y, 1), z, c)).start()
     remote(l_mine, l_mine, l_s.at[1], l_r.at[3], device(x, turn(y, -1), z, c)).start()
     remote(l_mine, l_mine, lt_s.at[0], lt_r.at[0], twin).start()
@@ -256,6 +255,7 @@
     right_further()
     left_further()
 
+    out[...] = jnp.zeros_like(out)
     gram_at = {}
     row = 5
     for k in range(4):
@@ -408,6 +408,16 @@
         rows = pl.ds(pl.multiple_of(g * 256, 256), 256)
         right_block(g, 0)
         right_block(g, 3)
+        right_block(g, 1)
+        right_block(g, 2)
+
+        @pl.when(i < 3)
+        def _():
+            rs_out[0, i] = out[rows, 256:512].astype(jnp.bfloat16)
+            remote(
+                rs_out.at[0, i], rs_in.at[0, i], rs_s.at[i], rs_r.at[i], device(g, y, z, c)
+            ).start()
+
         halo_out[0, rows] = out[rows, 0:128].astype(jnp.bfloat16)
         halo_out[1, rows] = out[rows, 640:768].astype(jnp.bfloat16)
         remote(
@@ -416,15 +426,6 @@
         remote(
             halo_out.at[1, rows], halo_in.at[0, rows], halo_s.at[4 + i], halo_r.at[i], right_next
         ).start()
-        right_block(g, 1)
-        right_block(g, 2)
-
-        @pl.when(i < 3)
-        def _():
-            rs_out[0, i] = out[rows, 256:512].astype(jnp.bfloat16)
-            remote(
-                rs_out.at[0, i], rs_in.at[0, i], rs_s.at[i], rs_r.at[i], device(g, y, z, c)
-            ).start()
 
         return carry
 

time: 70.6 us -> 70.2 us (level)
  no operation moved by 1% of the time
where the time goes in v8:
time: 70.2 us; the launch traced here: 70 us
  Pallas kernels  69.4 us (99%)
    pallas_call x1, Pallas kernels, per_device(): pl.pallas_call(kernel, out_shape=(shape, jax.ShapeDtypeStruct((8, 128), f...  67.2 us
    pallas_call x1, Pallas kernels, per_device(): pl.pallas_call(write_kernel, grid=(1024 // each,), out_shape=(shape, shap...  2.21 us

profile of v8, /device:TPU:1, one launch (start us, length us, event | category | flops | bytes accessed | tf_op | source)
XLA Modules:
  0.0 70.0 jit_solution(15173558713741776564)
XLA Ops:
  0.6 67.2 %two_site_step.1 = (f32[1024,128]{1,0:T(8,128)}, f32[8,128]{1,0:T(8,128)}) custom-call(s32[64]{0:T(128)} %lsec.1, s32[64]{0:T(128)} %rsec.1, s32[9,32]{1,0:T(8,128)} %terms.1, bf16[128,4096]{1,0:T(8,128)(2,1)} %psi.1, bf16[4,1024,128]{2,1,0:T(8,128)(2,1)} %sub_ref.1, bf16[9,320,128]{2,1,0:T(8,128)(2,1)} %bitcast.2, bf16[9,320,128]{2,1,0:T(8,128)(2,1)} %bitcast.3), custom_call_target="tpu_custom_call" | custom-call | tf_op jit(solution)/shard_map/two_site_step/pallas_call | solution.py:607
  67.8 2.2 %write_results.1 = (f32[1024,128]{1,0:T(8,128)}, f32[1024,128]{1,0:T(8,128)}) custom-call(f32[8,128]{1,0:T(8,128)} %get-tuple-element.4.stats_ref, f32[1024,128]{1,0:T(8,128)} %get-tuple-element.5.app_ref, bf16[4,1024,128]{2,1,0:T(8,128)(2,1)} %sub_ref.1), custom_call_target="tpu_custom_call" | custom-call | tf_op jit(solution)/shard_map/write_results/pallas_call | solution.py:646
